TPU v7x, 256 devices: a whole 4x4x8 slice. The times are simulated.
256 devices in a mesh: gx: 8 (over y, core), gy: 32 (over x, z).
Axes of the slice: x: 4, y: 4, z: 8, core: 2. Of those that a mesh axis runs over, the one named last changes fastest.
Arguments:
- right_side: float32 [6, 33, 128, 1024], P(None, None, 'gy', 'gx'), may hold values from -12 to 12
- base_flow: float32 [2, 33, 128, 1024], P(None, None, 'gy', 'gx'), may hold values from -4 to 4
- relax: float32 [128, 1024], P('gy', 'gx'), may hold values from 0.4 to 4
Outputs:
- solution_field: float32 [6, 33, 128, 1024], P(None, None, 'gy', 'gx')
- residual: float32 [6, 33, 128, 1024], P(None, None, 'gy', 'gx')
All inputs are finite; a program needn't handle non-finite values.
Results may differ from a plain program's by a relative error of at most 0.0044.
Values sent between devices are 32-bit elements; how exact they have to be, the bound alone decides.
No kernel may reach another device: no remote copies, remote signals or barrier semaphores. Data moves between devices by JAX's collectives and lax.ppermute only.
A program may use at most 64 MiB of HBM per device.

v0:
```python
import jax
import jax.numpy as jnp
import numpy as np
from jax import lax
from jax.experimental import pallas as pl
from jax.experimental.pallas import tpu as pltpu
from jax.sharding import PartitionSpec as P

F = 6
T = 33
TP = 40
R = 4
H = 4
E = R + 2 * H
NV = 9
SHIFT = 0.5
SCALE = 0.46
STEP = SCALE / 3.0
MOVE = SCALE * SHIFT
TIMED = (0, 1, 3, 4, 5)
PAIRS = [(i, j) for i in range(NV) for j in range(i, NV)]
EARLY = [(i, j) for i, j in PAIRS if j < 5]
PEERS = 256
SIDE = 2 * TP
FLOW = 208
VM = pl.BlockSpec(memory_space=pltpu.VMEM)


def time_matrices():
    index = np.arange(T, dtype=np.float64)
    diff = index[:, None] - index[None, :]
    sines = np.where(diff == 0.0, 1.0, np.sin(np.pi * diff / T))
    dmat = np.where(diff == 0.0, 0.0, 0.5 * np.where(diff % 2 == 0, 1.0, -1.0) / sines)
    mats = []
    for diagonal in (0.4 * STEP - MOVE, -MOVE):
        full = np.zeros((TP, TP), np.float32)
        full[:T, :T] = 0.8 * STEP * dmat + diagonal * np.eye(T)
        high = full.astype(jnp.bfloat16)
        low = (full - high.astype(np.float32)).astype(jnp.bfloat16)
        top = np.concatenate([high, high], 1)
        bottom = np.concatenate([low, np.zeros_like(low)], 1)
        mats.append(np.concatenate([top, bottom], 0))
    return np.stack(mats)


def lanes(shape=(1, 128)):
    return lax.broadcasted_iota(jnp.int32, shape, len(shape) - 1)


def window(x, place):
    lane = lanes()
    return jnp.where((lane >= place) & (lane < place + 8), pltpu.roll(x, (place + 4) % 128, 1), 0.0)


def raw(ref, f, r):
    return ref[pl.ds(f * T * R + r, T, stride=R), :]


def is_odd():
    return lax.rem(lax.axis_index("gy"), 2) == 1


def pack_kernel(rs, flow, relax, mats_in, message, even, odd, pack, mats, sems):
    rows = F * T * R
    copies = [
        pltpu.make_async_copy(rs, message.at[pl.ds(0, rows)], sems.at[0]),
        pltpu.make_async_copy(flow, message.at[pl.ds(rows, 2 * T * R)], sems.at[1]),
        pltpu.make_async_copy(relax, message.at[pl.ds(8 * T * R, R)], sems.at[2]),
        pltpu.make_async_copy(mats_in, mats, sems.at[3]),
    ]
    for copy in copies:
        copy.start()
    for copy in copies:
        copy.wait()
    for to in (even, odd):
        to[pl.ds(SIDE + FLOW - 8, 8), :] = jnp.zeros((8, 128), jnp.float32)
    for g in range(2):
        total = jnp.zeros((T, 128), jnp.float32)
        for j in range(4):
            for r in range(R):
                total = total + window(raw(message, g * 4 + j, r), j * 32 + r * 8)
        pack[g * TP : g * TP + 32, :] = total[0:32]
        last = jnp.zeros((8, 128), jnp.float32)
        sub = lax.broadcasted_iota(jnp.int32, (8, 128), 0)
        last = jnp.where(sub == 0, jnp.broadcast_to(total[32:33], (8, 128)), last)
        if g == 1:
            extra = jnp.zeros((1, 128), jnp.float32)
            for r in range(R):
                extra = extra + window(message[pl.ds(8 * T * R + r, 1), :], 2 * 32 + r * 8)
            last = jnp.where(sub == 1, jnp.broadcast_to(extra, (8, 128)), last)
        pack[g * TP + 32 : g * TP + 40, :] = last

    def rows_for(to, first):
        for j in range(2):
            for q in range(H - 1):
                to[pl.ds(SIDE + (j * (H - 1) + q) * T, T), :] = raw(message, F + j, first + q)
        for q in range(H - 1):
            to[pl.ds(SIDE + 2 * (H - 1) * T + q, 1), :] = message[pl.ds(8 * T * R + first + q, 1), :]

    @pl.when(is_odd())
    def _():
        rows_for(even, 0)
        rows_for(odd, 1)

    @pl.when(jnp.logical_not(is_odd()))
    def _():
        rows_for(even, 1)
        rows_for(odd, 0)


def put(dst, index, x, scale=None):
    dst[index + (pl.ds(32, 8), slice(None))] = jnp.zeros((8, 128), jnp.float32)
    dst[index + (pl.ds(0, T), slice(None))] = x if scale is None else x * scale


def slabs_of(ref):
    return [ref.at[pl.ds(g * TP, TP)] for g in range(2)]


def sides_of(dst, f, own, sides, g, j, ok):
    lane = lanes()
    north, here, south = (
        pltpu.roll(ref[g][...], (base - 32 * j) % 128, 1) for base, ref in zip((0, 32, 64), sides)
    )
    halo = jnp.where(lane < 32, north, jnp.where(lane < 64, here, south))
    slot = lane % 8
    dst[f, 0] = jnp.where(slot < 4, halo, own) * ok[0]
    dst[f, 1] = jnp.where(slot < 4, own, halo) * ok[1]


def own_windows(slab, rows=range(E)):
    total = jnp.zeros((TP, 128), jnp.float32)
    for e in rows:
        total = total + window(slab(e), e * 8)
    return total


def fill(own, north, south, sides, ext, side):
    ok_north, ok_south, _, _ = masks()
    ok = side_masks((1, 128))
    for f in range(F):
        for r in range(R):
            put(ext, (f, r), raw(north, f, r), ok_north)
            put(ext, (f, H + r), raw(own, f, r))
            put(ext, (f, H + R + r), raw(south, f, r), ok_south)
    for f in range(F):
        sides_of(side, f, own_windows(lambda e: ext[f, e]), sides, f // 4, f % 4, ok)


def masks():
    gx, gy = lax.axis_index("gx"), lax.axis_index("gy")
    north = jnp.where(gy > 0, 1.0, 0.0).astype(jnp.float32)
    south = jnp.where(gy < lax.axis_size("gy") - 1, 1.0, 0.0).astype(jnp.float32)
    west = jnp.where(gx > 0, 1.0, 0.0).astype(jnp.float32)
    east = jnp.where(gx < lax.axis_size("gx") - 1, 1.0, 0.0).astype(jnp.float32)
    return north, south, west, east


def side_masks(shape):
    north, south, west, east = masks()
    lane = lanes(shape)
    row, slot = lane // 8, lane % 8
    rows_ok = jnp.where(row < H, north, jnp.where(row < H + R, 1.0, jnp.where(row < E, south, 0.0)))
    return [rows_ok * jnp.where(slot < 4, west, 1.0), rows_ok * jnp.where(slot < 4, 1.0, east)]


def combine(core, xm, xp, ym, yp, fu, fv, rl, td):
    ex = [a - b for a, b in zip(xp, xm)]
    ey = [a - b for a, b in zip(yp, ym)]
    half = 0.5 * STEP
    carried = {f: td[f] + fu * ex[f] + fv * ey[f] for f in TIMED}
    around = [xp[f] + xm[f] + (yp[f] + ym[f]) for f in range(3)]
    return [
        carried[0] - (0.1 * STEP) * around[0] + half * (ex[2] - ex[3] - ey[4]),
        carried[1] - (0.1 * STEP) * around[1] + half * (ey[2] - ex[4] - ey[5]),
        half * (ex[0] + ey[1]) - (0.2 * STEP) * around[2] + (0.8 * STEP - MOVE) * core[2],
        carried[3] + rl * core[3] - half * ex[0],
        carried[4] + rl * core[4] - (0.5 * half) * (ey[0] + ex[1]),
        carried[5] + rl * core[5] - half * ey[1],
    ]


def steps(mats, exts, slabs, flow, sflow, td, std, merged, basis, first):
    north, south, _, _ = masks()
    side_ok = side_masks((8, 128))
    lane = lanes((8, 128))

    def timed(f, a, b):
        x = jnp.concatenate([a, b], 1)
        high = x.astype(jnp.bfloat16).astype(jnp.float32)
        both = jnp.concatenate([high, x - high], 0).astype(jnp.bfloat16)
        out = jnp.dot(mats[0 if f < 2 else 1], both, preferred_element_type=jnp.float32)
        out = out[:TP] + out[TP:]
        return out[:, :128], out[:, 128:]

    for k in range(H):
        src, dst = exts[k % 2], exts[1 - k % 2]
        side, side_new = slabs[k % 2], slabs[1 - k % 2]
        low, count = k + 1, E - 2 * (k + 1)
        last = k == H - 1

        def time_pair(r, src=src):
            for n, f in enumerate(TIMED):
                td[n, r], td[n, r + 1] = timed(f, src[f, r], src[f, r + 1])

        def main_pair(r, src=src, dst=dst):
            keep = [jnp.where(e < H, north, jnp.where(e < H + R, jnp.float32(1.0), south)) for e in (r, r + 1)]
            for c in range(TP // 8):
                s = pl.ds(8 * c, 8)
                rows = [[src[f, r + e, s] for f in range(F)] for e in (-1, 0, 1, 2)]
                beside = [merged[f, s] for f in range(F)]
                for e in range(2):
                    xm, core, xp = rows[e : e + 3]
                    edge = [pltpu.roll(a, 125 - 8 * (r + e), 1) for a in beside]
                    ym = [jnp.where(lane == 0, b, pltpu.roll(a, 1, 1)) for a, b in zip(core, edge)]
                    yp = [jnp.where(lane == 127, b, pltpu.roll(a, 127, 1)) for a, b in zip(core, edge)]
                    rl = jnp.broadcast_to(flow[0, r + e, pl.ds(T, 1)], (8, 128))
                    times = {f: td[n, r + e, s] for n, f in enumerate(TIMED)}
                    out = combine(core, xm, xp, ym, yp, flow[0, r + e, s], flow[1, r + e, s], rl, times)
                    for f in range(F):
                        dst[f, r + e, s] = out[f] * keep[e]

        def pair(i, carry, low=low, time_pair=time_pair, main_pair=main_pair):
            r = low + 2 * i
            time_pair(jnp.minimum(r + 2, E - 2))
            main_pair(r)
            return carry

        for f in range(F):
            merged[f] = jnp.where(lanes() % 8 == 3, side[f, 0], pltpu.roll(side[f, 1], 126, 1))
        if not last:
            for n, f in enumerate(TIMED):
                std[n, 0], std[n, 1] = timed(f, side[f, 0], side[f, 1])
        time_pair(low)
        lax.fori_loop(0, count // 2, pair, 0, unroll=True)
        for p in range(0 if last else 2):
            for c in range(TP // 8):
                s = pl.ds(8 * c, 8)
                core = [side[f, p, s] for f in range(F)]
                xm, xp, ym, yp = ([pltpu.roll(a, by, 1) for a in core] for by in (8, 120, 1, 127))
                rl = jnp.broadcast_to(sflow[0, p, pl.ds(T, 1)], (8, 128))
                times = {f: std[n, p, s] for n, f in enumerate(TIMED)}
                out = combine(core, xm, xp, ym, yp, sflow[0, p, s], sflow[1, p, s], rl, times)
                for f in range(F):
                    side_new[f, p, s] = out[f] * side_ok[p]
        for f in range(F):
            for r in range(R):
                basis[first + k, f * R + r] = dst[f, H + r]


def by_parity(load, *pairs):
    @pl.when(is_odd())
    def _():
        load(*[pair[0] for pair in pairs], *[pair[1] for pair in pairs])

    @pl.when(jnp.logical_not(is_odd()))
    def _():
        load(*[pair[1] for pair in pairs], *[pair[0] for pair in pairs])


def first_kernel(own, even, odd, here, near_even, near_odd, mats, main, pack, basis, flow, sflow, ext0, ext1, side0, side1, td, std, merged):
    half = 0.5 * STEP

    def load(north, flow_north, south, flow_south):
        sides = [slabs_of(ref) for ref in (flow_north, here, flow_south)]
        fill(own, north, south, sides, ext0, side0)
        for j in range(2):
            for r in range(R):
                put(flow, (j, H + r), raw(own, F + j, r), half)
            for q in range(H - 1):
                place = pl.ds(SIDE + (j * (H - 1) + q) * T, T)
                put(flow, (j, 1 + q), flow_north[place, :], half)
                put(flow, (j, H + R + q), flow_south[place, :], half)
        for r in range(R):
            flow[0, H + r, pl.ds(T, 1), :] = own[pl.ds(8 * T * R + r, 1), :] * STEP
        for q in range(H - 1):
            place = pl.ds(SIDE + 2 * (H - 1) * T + q, 1)
            flow[0, 1 + q, pl.ds(T, 1), :] = flow_north[place, :] * STEP
            flow[0, H + R + q, pl.ds(T, 1), :] = flow_south[place, :] * STEP
        sub = lax.broadcasted_iota(jnp.int32, (TP, 128), 0)
        scale = jnp.where(sub == T, STEP, half).astype(jnp.float32)
        slot = lanes() % 8
        for j in range(2):
            sides_of(sflow, j, own_windows(lambda e: flow[j, e], range(1, E - 1)), sides, 1, 2 + j, (1.0, 1.0))
            for p in range(2):
                halo = (slot < 4) if p == 0 else (slot >= 4)
                sflow[j, p] = sflow[j, p] * jnp.where(halo, scale, 1.0)

    by_parity(load, (even, odd), (near_even, near_odd))
    for f in range(F):
        for r in range(R):
            basis[0, f * R + r] = ext0[f, H + r]
    steps(mats, (ext0, ext1), (side0, side1), flow, sflow, td, std, merged, basis, 1)
    for f in range(F):
        for r in range(R):
            main[pl.ds(f * T * R + r, T, stride=R), :] = basis[H, f * R + r, 0:T]
    for g in range(2):
        total = jnp.zeros((TP, 128), jnp.float32)
        for j in range(4 if g == 0 else 2):
            for r in range(R):
                total = total + window(basis[H, (g * 4 + j) * R + r], j * 32 + r * 8)
        pack[g * TP : (g + 1) * TP, :] = total


def products(slabs, pairs):
    def slab(i, sums):
        sums = list(sums)
        for c in range(TP // 8):
            s = pl.ds(8 * c, 8)
            vec = [get(i, s) for get in slabs]
            for e, (a, b) in enumerate(pairs):
                sums[e] = sums[e] + vec[a] * vec[b]
        return tuple(sums)

    zero = jnp.zeros((8, 128), jnp.float32)
    return lax.fori_loop(0, F * R, slab, (zero,) * len(pairs), unroll=2)


def gram_kernel(older, early):
    slabs = [lambda i, s, k=k: older[k, i, s] for k in range(5)]
    for e, value in enumerate(products(slabs, EARLY)):
        early[e] = value


def second_kernel(own, even, odd, here, corner_even, corner_odd, flow, sflow, older, early, mats, basis, gram, ext0, ext1, side0, side1, td, std, merged, rows):

    def load(north, above, south, below):
        fill(own, north, south, [slabs_of(ref) for ref in (above, here, below)], ext0, side0)

    by_parity(load, (even, odd), (corner_even, corner_odd))
    steps(mats, (ext0, ext1), (side0, side1), flow, sflow, td, std, merged, basis, 0)

    late = [pair for pair in PAIRS if pair not in EARLY]
    slabs = [lambda i, s, k=k: older[k, i, s] for k in range(5)] + [lambda i, s, k=k: basis[k, i, s] for k in range(4)]
    sums = dict(zip(late, products(slabs, late)))
    for e, pair in enumerate(EARLY):
        sums[pair] = early[e]
    rows[...] = jnp.zeros((48, 128), jnp.float32)
    for e, pair in enumerate(PAIRS):
        rows[pl.ds(e, 1), :] = jnp.sum(sums[pair], axis=0, keepdims=True)
    total = jnp.sum(rows[...], axis=1, keepdims=True)
    pick = lanes((48, 128)) == lax.broadcasted_iota(jnp.int32, (48, 128), 0)
    line = jnp.sum(jnp.where(pick, total, 0.0), axis=0, keepdims=True)
    gram[...] = jnp.broadcast_to(line, (PEERS, 128))


def plus(a, b):
    return b if a is None else a if b is None else a + b


def minus(a, b):
    return a if b is None else -b if a is None else a - b


def times(a, b):
    return None if a is None or b is None else a * b


def cycle(gram, c):
    q = [c]
    for _ in range(4):
        q.append([None] + q[-1][:-1])
    w = [
        [plus(times(2.0 + 3.0 * SHIFT, a), times(3.0 / SCALE, b)) for a, b in zip(q[k], q[k + 1])]
        for k in range(4)
    ]

    def dot(a, b):
        total = None
        for x, y in zip(a, b):
            total = plus(total, times(x, y))
        return total

    gw = [[dot(gram[i], v) for i in range(NV)] for v in w]
    n = 4
    y = [dot(c, gw[i]) for i in range(n)]
    low, inverse = [[None] * n for _ in range(n)], []
    for j in range(n):
        held = [dot(w[i], gw[j]) for i in range(j, n)]
        for m in range(j):
            scaled = low[j][m] * diag[m]
            held = [v - low[i][m] * scaled for i, v in zip(range(j, n), held)]
        diag = (diag if j else []) + [held[0]]
        inverse.append(1.0 / held[0])
        low[j][j] = 1.0
        for i in range(j + 1, n):
            low[i][j] = held[i - j] * inverse[j]
    for i in range(n):
        for m in range(i):
            y[i] = y[i] - low[i][m] * y[m]
    y = [a * b for a, b in zip(y, inverse)]
    for i in reversed(range(n)):
        for m in range(i + 1, n):
            y[i] = y[i] - low[m][i] * y[m]
    step, rest = [None] * NV, list(c)
    for i in range(n):
        step = [plus(a, times(y[i], b)) for a, b in zip(step, q[i])]
        rest = [minus(a, times(y[i], b)) for a, b in zip(rest, w[i])]
    return step, rest


def last_kernel(parts, older, newer, solution, residual):
    total = jnp.sum(parts[...].reshape(PEERS // 8, 8, 128), axis=0)
    total = jnp.sum(total, axis=0, keepdims=True)
    gram = [[None] * NV for _ in range(NV)]
    for e, (i, j) in enumerate(PAIRS):
        gram[i][j] = gram[j][i] = jnp.broadcast_to(total[:, e : e + 1], (8, 128))
    step1, rest = cycle(gram, [1.0] + [None] * (NV - 1))
    zero = jnp.zeros((8, 128), jnp.float32)
    rest = [zero if a is None else a for a in rest]
    step2, rest = cycle(gram, rest)
    step = [plus(a, b) for a, b in zip(step1, step2)]
    step = [None if a is None else a[0:1] for a in step]
    rest = [a[0:1] for a in rest]

    def slab(i, carry):
        f, r = i // R, i % R
        sol = res = None
        for k in range(NV):
            x = older[k, i, 0:T] if k < 5 else newer[k - 5, i, 0:T]
            if step[k] is not None:
                sol = plus(sol, step[k] * x)
            res = plus(res, rest[k] * x)
        solution[pl.ds(f * T * R + r, T, stride=R), :] = sol
        residual[pl.ds(f * T * R + r, T, stride=R), :] = res
        return carry

    lax.fori_loop(0, F * R, slab, 0)


def call(kernel, args, outs, scratch=(), first=False, final=False):
    space = pltpu.HBM if first else pltpu.VMEM
    args = [pltpu.with_memory_space_constraint(a, space) for a in args]
    make = jax.ShapeDtypeStruct if final else pltpu.VMEM
    kinds = [jnp.bfloat16 if shape[-1] == 2 * TP else jnp.float32 for shape in outs]
    scratch = [pltpu.VMEM(shape, jnp.float32) for shape in scratch]
    return pl.pallas_call(
        kernel,
        out_shape=[make(shape, kind) for shape, kind in zip(outs, kinds)],
        in_specs=[pl.BlockSpec(memory_space=space)] * len(args),
        out_specs=[VM] * len(outs),
        scratch_shapes=scratch + [pltpu.SemaphoreType.DMA((4,))] * first,
        compiler_params=pltpu.CompilerParams(vmem_limit_bytes=24 << 20),
    )(*args)


def trades(across, down):
    even = [(g * down + j, g * down + (j ^ 1)) for g in range(across) for j in range(down)]
    odd = []
    for g in range(across):
        for j in range(down):
            edge = j in (0, down - 1)
            other = j if edge else j + 1 if j % 2 else j - 1
            odd.append((g * down + j, (g ^ 1 if edge else g) * down + other))
    return even, odd


def exchange(rows, pack, behind=()):
    across = lax.axis_size("gx")
    pairs = trades(across, lax.axis_size("gy"))
    axes = ("gx", "gy")
    rows = [lax.ppermute(rows, axes, p) for p in pairs]
    left = lax.ppermute(pack, "gx", [(g, (g + 1) % across) for g in range(across)])
    right = lax.ppermute(pack, "gx", [((g + 1) % across, g) for g in range(across)])
    slot = lax.broadcasted_iota(jnp.int32, pack.shape, 1) % 8
    here = jnp.where(slot < 4, left, right)
    near = [x.at[:SIDE].set(here) for x in behind] or [here, here]
    corners = [lax.ppermute(x, axes, p) for x, p in zip(near, pairs)]
    return *rows, here, *corners


WORK = (
    (F, E, TP, 128),
    (F, E, TP, 128),
    (F, 2, TP, 128),
    (F, 2, TP, 128),
    (len(TIMED), E, TP, 128),
    (len(TIMED), 2, TP, 128),
    (F, TP, 128),
)


def shards(right_side, base_flow, relax):
    rs = right_side.reshape(F * T * R, 128)
    flow = base_flow.reshape(2 * T * R, 128)
    own, to_even, to_odd, pack, mats = call(
        pack_kernel,
        (rs, flow, relax, jnp.asarray(time_matrices())),
        ((8 * T * R + 8, 128), (SIDE + FLOW, 128), (SIDE + FLOW, 128), (SIDE, 128), (2, 2 * TP, 2 * TP)),
        first=True,
    )
    own, pack, older, flows, side_flows = call(
        first_kernel,
        (own, *exchange(rs, pack, (to_even, to_odd)), mats),
        ((F * T * R, 128), (2 * TP, 128), (5, F * R, TP, 128), (2, E, TP, 128), (2, 2, TP, 128)),
        WORK,
    )
    (early,) = call(gram_kernel, (older,), ((len(EARLY), 8, 128),))
    newer, gram = call(
        second_kernel,
        (own, *exchange(own, pack), flows, side_flows, older, early, mats),
        ((4, F * R, TP, 128), (PEERS, 128)),
        WORK + ((48, 128),),
    )
    parts = lax.all_to_all(gram.reshape(PEERS, 1, 128), ("gx", "gy"), 0, 0, tiled=True)
    solution_field, residual = call(
        last_kernel,
        (parts.reshape(PEERS, 128), older, newer),
        ((F * T * R, 128), (F * T * R, 128)),
        final=True,
    )
    return solution_field.reshape(right_side.shape), residual.reshape(right_side.shape)


def solution(mesh):
    placed = (P(None, None, "gy", "gx"), P(None, None, "gy", "gx"), P("gy", "gx"))
    return jax.shard_map(
        shards,
        mesh=mesh,
        in_specs=placed,
        out_specs=(P(None, None, "gy", "gx"), P(None, None, "gy", "gx")),
        check_vma=False,
    )
```

profile of v0, /device:TPU:1, one launch (start us, length us, event | category | flops | bytes accessed | tf_op | source)
XLA Modules:
  0.0 72.0 jit_solution(6146885125312987553)
XLA Ops:
  0.6 3.3 %collective-permute-start.1 = (f32[792,128]{1,0:T(8,128)}, f32[792,128]{1,0:T(8,128)S(1)}, u32[]{:S(2)}, u32[]{:S(2)}) collective-permute-start(f32[792,128]{1,0:T(8,128)} %bitcast.10), channel_id=1, source_target_pairs={{0,32},{1,2},{2,1},{3,4},{4,3},{5,6},{6,5},{7,8},{8,7},{9,10},{10,... | collective-permute-start | bytes 1216520 | tf_op jit(solution)/shard_map/ppermute | solution.py:462
  4.0 0.9 %collective-permute-start = (f32[792,128]{1,0:T(8,128)}, f32[792,128]{1,0:T(8,128)S(1)}, u32[]{:S(2)}, u32[]{:S(2)}) collective-permute-start(f32[792,128]{1,0:T(8,128)} %bitcast.11), channel_id=1, source_target_pairs={{0,1},{1,0},{2,3},{3,2},{4,5},{5,4},{6,7},{7,6},{8,9},{9,8},{10,11... | collective-permute-start | bytes 1216520 | tf_op jit(solution)/shard_map/ppermute | solution.py:462
  4.8 1.3 %shard_map.59 = (f32[1064,128]{1,0:T(8,128)S(1)}, f32[288,128]{1,0:T(8,128)S(1)}, f32[288,128]{1,0:T(8,128)S(1)}, f32[80,128]{1,0:T(8,128)S(1)}, bf16[2,80,80]{2,1,0:T(8,128)(2,1)S(1)}) custom-call(f32[792,128]{1,0:T(8,128)} %bitcast.12, f32[264,128]{1,0:T(8,128)} %bitcast.13, f32[4,128]{1,0:T(4,128)} %relax.1, bf16[2,80,80]{2,1,0:T(8,128)(2,1)} %constant.70.clone.mats_in), custom_call_target="tpu_custom_call" | custom-call | tf_op jit(solution)/shard_map/pallas_call | solution.py:437
  6.2 1.2 %collective-permute-start.3 = (f32[80,128]{1,0:T(8,128)S(1)}, f32[80,128]{1,0:T(8,128)S(1)}, u32[]{:S(2)}, u32[]{:S(2)}) collective-permute-start(f32[80,128]{1,0:T(8,128)S(1)} %get-tuple-element.41), channel_id=1, source_target_pairs={{32,0},{64,32},{96,64},{128,96},{160,128},{192,160},{224,192},{0,2... | collective-permute-start | bytes 122888 | tf_op jit(solution)/shard_map/ppermute | solution.py:464
  7.4 1.2 %collective-permute-start.2 = (f32[80,128]{1,0:T(8,128)S(1)}, f32[80,128]{1,0:T(8,128)S(1)}, u32[]{:S(2)}, u32[]{:S(2)}) collective-permute-start(f32[80,128]{1,0:T(8,128)S(1)} %get-tuple-element.41), channel_id=1, source_target_pairs={{0,32},{32,64},{64,96},{96,128},{128,160},{160,192},{192,224},{224... | collective-permute-start | bytes 122888 | tf_op jit(solution)/shard_map/ppermute | solution.py:463
  8.6 1.9 %collective-permute-done.3 = f32[80,128]{1,0:T(8,128)S(1)} collective-permute-done((f32[80,128]{1,0:T(8,128)S(1)}, f32[80,128]{1,0:T(8,128)S(1)}, u32[]{:S(2)}, u32[]{:S(2)}) %collective-permute-start.3) | collective-permute-done | bytes 40992 | tf_op jit(solution)/shard_map/ppermute | solution.py:464
  10.6 0.1 collective-permute-start.4
  10.7 3.6 %collective-permute-start.5 = (f32[288,128]{1,0:T(8,128)S(1)}, f32[288,128]{1,0:T(8,128)S(1)}, u32[]{:S(2)}, u32[]{:S(2)}) collective-permute-start(f32[288,128]{1,0:T(8,128)S(1)} %get-tuple-element.54), channel_id=1, source_target_pairs={{0,32},{1,2},{2,1},{3,4},{4,3},{5,6},{6,5},{7,8},{8,7},{9,10},{10,... | collective-permute-start | bytes 442376 | tf_op jit(solution)/shard_map/ppermute | solution.py:468
  14.4 2.5 %collective-permute-done.4.near_even = f32[288,128]{1,0:T(8,128)S(1)} collective-permute-done((f32[288,128]{1,0:T(8,128)S(1)}, f32[288,128]{1,0:T(8,128)S(1)}, u32[]{:S(2)}, u32[]{:S(2)}) %collective-permute-start.4) | collective-permute-done | bytes 147488 | tf_op jit(solution)/shard_map/ppermute | solution.py:468
  16.9 0.0 collective-permute-done.5.near_odd
  16.9 5.3 %shard_map.60 = (f32[792,128]{1,0:T(8,128)S(1)}, f32[80,128]{1,0:T(8,128)S(1)}, f32[5,24,40,128]{3,2,1,0:T(8,128)S(1)}, f32[2,12,40,128]{3,2,1,0:T(8,128)S(1)}, f32[2,2,40,128]{3,2,1,0:T(8,128)S(1)}) custom-call(f32[1064,128]{1,0:T(8,128)S(1)} %get-tuple-element.40.own, f32[792,128]{1,0:T(8,128)S(1)} %collective-permute-done.even, ...), custom_call_target="tpu_custom_call" | custom-call | tf_op jit(solution)/shard_map/pallas_call | solution.py:437
  22.2 2.4 %collective-permute-start.7 = (f32[792,128]{1,0:T(8,128)S(1)}, f32[792,128]{1,0:T(8,128)S(1)}, u32[]{:S(2)}, u32[]{:S(2)}) collective-permute-start(f32[792,128]{1,0:T(8,128)S(1)} %get-tuple-element.45.own), channel_id=1, source_target_pairs={{0,32},{1,2},{2,1},{3,4},{4,3},{5,6},{6,5},{7,8},{8,7},{9,10},{10,... | collective-permute-start | bytes 1216520 | tf_op jit(solution)/shard_map/ppermute | solution.py:462
  24.6 1.6 %collective-permute-start.6 = (f32[792,128]{1,0:T(8,128)S(1)}, f32[792,128]{1,0:T(8,128)S(1)}, u32[]{:S(2)}, u32[]{:S(2)}) collective-permute-start(f32[792,128]{1,0:T(8,128)S(1)} %get-tuple-element.45.own), channel_id=1, source_target_pairs={{0,1},{1,0},{2,3},{3,2},{4,5},{5,4},{6,7},{7,6},{8,9},{9,8},{10,11... | collective-permute-start | bytes 1216520 | tf_op jit(solution)/shard_map/ppermute | solution.py:462
  26.2 3.7 %collective-permute-start.9 = (f32[80,128]{1,0:T(8,128)S(1)}, f32[80,128]{1,0:T(8,128)S(1)}, u32[]{:S(2)}, u32[]{:S(2)}) collective-permute-start(f32[80,128]{1,0:T(8,128)S(1)} %get-tuple-element.46), channel_id=1, source_target_pairs={{32,0},{64,32},{96,64},{128,96},{160,128},{192,160},{224,192},{0,2... | collective-permute-start | bytes 122888 | tf_op jit(solution)/shard_map/ppermute | solution.py:464
  29.9 0.3 collective-permute-start.8
  30.2 2.0 %collective-permute-done.9 = f32[80,128]{1,0:T(8,128)S(1)} collective-permute-done((f32[80,128]{1,0:T(8,128)S(1)}, f32[80,128]{1,0:T(8,128)S(1)}, u32[]{:S(2)}, u32[]{:S(2)}) %collective-permute-start.9) | collective-permute-done | bytes 40992 | tf_op jit(solution)/shard_map/ppermute | solution.py:464
  32.2 2.6 %collective-permute-start.11 = (f32[80,128]{1,0:T(8,128)S(1)}, f32[80,128]{1,0:T(8,128)S(1)}, u32[]{:S(2)}, u32[]{:S(2)}) collective-permute-start(f32[80,128]{1,0:T(8,128)S(1)} %fusion.here), channel_id=1, source_target_pairs={{0,32},{1,2},{2,1},{3,4},{4,3},{5,6},{6,5},{7,8},{8,7},{9,10},{10,... | collective-permute-start | bytes 122888 | tf_op jit(solution)/shard_map/ppermute | solution.py:468
  34.7 0.1 collective-permute-start.10
  34.9 0.5 shard_map.61.early
  35.4 0.2 collective-permute-done.11.corner_odd
  35.6 2.0 %collective-permute-done.10.corner_even = f32[80,128]{1,0:T(8,128)S(1)} collective-permute-done((f32[80,128]{1,0:T(8,128)S(1)}, f32[80,128]{1,0:T(8,128)S(1)}, u32[]{:S(2)}, u32[]{:S(2)}) %collective-permute-start.10) | collective-permute-done | bytes 40992 | tf_op jit(solution)/shard_map/ppermute | solution.py:468
  37.6 6.4 %shard_map.62 = (f32[4,24,40,128]{3,2,1,0:T(8,128)S(1)}, f32[256,128]{1,0:T(8,128)S(1)}) custom-call(f32[792,128]{1,0:T(8,128)S(1)} %get-tuple-element.45.own, f32[792,128]{1,0:T(8,128)S(1)} %collective-permute-done.6.even, f32[792,128]{1,0:T(8,128)S(1)} %collective-permute-done.7.odd, f32[80,128]{1,0:T(8,128)S(1)} %fusion.here, ...), custom_call_target="tpu_custom_call" | custom-call | tf_op jit(solution)/shard_map/pallas_call | solution.py:437
  44.0 26.1 %all_to_all.5 = f32[256,1,128]{2,1,0:T(1,128)S(1)} all-to-all(f32[256,1,128]{2,1,0:T(1,128)S(1)} %bitcast.9), channel_id=1, replica_groups=mesh['gx'=8,'gy'=32] {'gx','gy'}, dimensions={0} | all-to-all | bytes 262144 | tf_op jit(solution)/shard_map/all_to_all | solution.py:505
  70.1 2.0 %shard_map.63 = (f32[792,128]{1,0:T(8,128)}, f32[792,128]{1,0:T(8,128)}) custom-call(f32[256,128]{1,0:T(8,128)S(1)} %bitcast.8, f32[5,24,40,128]{3,2,1,0:T(8,128)S(1)} %get-tuple-element.49.older, f32[4,24,40,128]{3,2,1,0:T(8,128)S(1)} %get-tuple-element.51.newer), custom_call_target="tpu_custom_call" | custom-call | tf_op jit(solution)/shard_map/pallas_call | solution.py:437
  (11 shorter events, 0.0 us)
Async XLA Ops:
  0.6 16.2 %collective-permute-start.1 = (f32[792,128]{1,0:T(8,128)}, f32[792,128]{1,0:T(8,128)S(1)}, u32[]{:S(2)}, u32[]{:S(2)}) collective-permute-start(f32[792,128]{1,0:T(8,128)} %bitcast.10), channel_id=1, source_target_pairs={{0,32},{1,2},{2,1},{3,4},{4,3},{5,6},{6,5},{7,8},{8,7},{9,10},{10,... | collective-permute-start | bytes 1216520 | tf_op jit(solution)/shard_map/ppermute | solution.py:462
  4.0 12.9 %collective-permute-start = (f32[792,128]{1,0:T(8,128)}, f32[792,128]{1,0:T(8,128)S(1)}, u32[]{:S(2)}, u32[]{:S(2)}) collective-permute-start(f32[792,128]{1,0:T(8,128)} %bitcast.11), channel_id=1, source_target_pairs={{0,1},{1,0},{2,3},{3,2},{4,5},{5,4},{6,7},{7,6},{8,9},{9,8},{10,11... | collective-permute-start | bytes 1216520 | tf_op jit(solution)/shard_map/ppermute | solution.py:462
  6.2 4.4 %collective-permute-start.3 = (f32[80,128]{1,0:T(8,128)S(1)}, f32[80,128]{1,0:T(8,128)S(1)}, u32[]{:S(2)}, u32[]{:S(2)}) collective-permute-start(f32[80,128]{1,0:T(8,128)S(1)} %get-tuple-element.41), channel_id=1, source_target_pairs={{32,0},{64,32},{96,64},{128,96},{160,128},{192,160},{224,192},{0,2... | collective-permute-start | bytes 122888 | tf_op jit(solution)/shard_map/ppermute | solution.py:464
  7.4 3.2 %collective-permute-start.2 = (f32[80,128]{1,0:T(8,128)S(1)}, f32[80,128]{1,0:T(8,128)S(1)}, u32[]{:S(2)}, u32[]{:S(2)}) collective-permute-start(f32[80,128]{1,0:T(8,128)S(1)} %get-tuple-element.41), channel_id=1, source_target_pairs={{0,32},{32,64},{64,96},{96,128},{128,160},{160,192},{192,224},{224... | collective-permute-start | bytes 122888 | tf_op jit(solution)/shard_map/ppermute | solution.py:463
  10.6 6.3 %collective-permute-start.4 = (f32[288,128]{1,0:T(8,128)S(1)}, f32[288,128]{1,0:T(8,128)S(1)}, u32[]{:S(2)}, u32[]{:S(2)}) collective-permute-start(f32[288,128]{1,0:T(8,128)S(1)} %constant_dynamic-update-slice_fusion.1), channel_id=1, source_target_pairs={{0,1},{1,0},{2,3},{3,2},{4,5},{5,4},{6,7},{7,6},{8,9},{9,8},{10,11... | collective-permute-start | bytes 442376 | tf_op jit(solution)/shard_map/ppermute | solution.py:468
  10.7 6.2 %collective-permute-start.5 = (f32[288,128]{1,0:T(8,128)S(1)}, f32[288,128]{1,0:T(8,128)S(1)}, u32[]{:S(2)}, u32[]{:S(2)}) collective-permute-start(f32[288,128]{1,0:T(8,128)S(1)} %get-tuple-element.54), channel_id=1, source_target_pairs={{0,32},{1,2},{2,1},{3,4},{4,3},{5,6},{6,5},{7,8},{8,7},{9,10},{10,... | collective-permute-start | bytes 442376 | tf_op jit(solution)/shard_map/ppermute | solution.py:468
  22.2 15.4 %collective-permute-start.7 = (f32[792,128]{1,0:T(8,128)S(1)}, f32[792,128]{1,0:T(8,128)S(1)}, u32[]{:S(2)}, u32[]{:S(2)}) collective-permute-start(f32[792,128]{1,0:T(8,128)S(1)} %get-tuple-element.45.own), channel_id=1, source_target_pairs={{0,32},{1,2},{2,1},{3,4},{4,3},{5,6},{6,5},{7,8},{8,7},{9,10},{10,... | collective-permute-start | bytes 1216520 | tf_op jit(solution)/shard_map/ppermute | solution.py:462
  24.6 13.0 %collective-permute-start.6 = (f32[792,128]{1,0:T(8,128)S(1)}, f32[792,128]{1,0:T(8,128)S(1)}, u32[]{:S(2)}, u32[]{:S(2)}) collective-permute-start(f32[792,128]{1,0:T(8,128)S(1)} %get-tuple-element.45.own), channel_id=1, source_target_pairs={{0,1},{1,0},{2,3},{3,2},{4,5},{5,4},{6,7},{7,6},{8,9},{9,8},{10,11... | collective-permute-start | bytes 1216520 | tf_op jit(solution)/shard_map/ppermute | solution.py:462
  26.2 6.0 %collective-permute-start.9 = (f32[80,128]{1,0:T(8,128)S(1)}, f32[80,128]{1,0:T(8,128)S(1)}, u32[]{:S(2)}, u32[]{:S(2)}) collective-permute-start(f32[80,128]{1,0:T(8,128)S(1)} %get-tuple-element.46), channel_id=1, source_target_pairs={{32,0},{64,32},{96,64},{128,96},{160,128},{192,160},{224,192},{0,2... | collective-permute-start | bytes 122888 | tf_op jit(solution)/shard_map/ppermute | solution.py:464
  29.9 2.2 %collective-permute-start.8 = (f32[80,128]{1,0:T(8,128)S(1)}, f32[80,128]{1,0:T(8,128)S(1)}, u32[]{:S(2)}, u32[]{:S(2)}) collective-permute-start(f32[80,128]{1,0:T(8,128)S(1)} %get-tuple-element.46), channel_id=1, source_target_pairs={{0,32},{32,64},{64,96},{96,128},{128,160},{160,192},{192,224},{224... | collective-permute-start | bytes 122888 | tf_op jit(solution)/shard_map/ppermute | solution.py:463
  32.2 3.4 %collective-permute-start.11 = (f32[80,128]{1,0:T(8,128)S(1)}, f32[80,128]{1,0:T(8,128)S(1)}, u32[]{:S(2)}, u32[]{:S(2)}) collective-permute-start(f32[80,128]{1,0:T(8,128)S(1)} %fusion.here), channel_id=1, source_target_pairs={{0,32},{1,2},{2,1},{3,4},{4,3},{5,6},{6,5},{7,8},{8,7},{9,10},{10,... | collective-permute-start | bytes 122888 | tf_op jit(solution)/shard_map/ppermute | solution.py:468
  34.7 2.9 %collective-permute-start.10 = (f32[80,128]{1,0:T(8,128)S(1)}, f32[80,128]{1,0:T(8,128)S(1)}, u32[]{:S(2)}, u32[]{:S(2)}) collective-permute-start(f32[80,128]{1,0:T(8,128)S(1)} %fusion.here), channel_id=1, source_target_pairs={{0,1},{1,0},{2,3},{3,2},{4,5},{5,4},{6,7},{7,6},{8,9},{9,8},{10,11... | collective-permute-start | bytes 122888 | tf_op jit(solution)/shard_map/ppermute | solution.py:468
where the time goes:
time: 72.2 us; the launch traced here: 72 us
  blocking collectives  26.1 us (36%)
  starting transfers between devices  21.1 us (29%)
  Pallas kernels  15.5 us (21%)
  waiting for transfers between devices  8.67 us (12%)
    all_to_all x1, blocking collectives, shards(): lax.all_to_all(gram.reshape(PEERS, 1, 128), ('gx', 'gy'), 0, 0, tiled=True)  26.1 us
    pallas_call x5, Pallas kernels, call(): pl.pallas_call(kernel, out_shape=[make(shape, kind) for shape, kind in zi...  15.5 us
    ppermute x4, starting transfers between devices, exchange(): rows = [lax.ppermute(rows, axes, p) for p in pairs]  8.18 us
    ppermute x4, starting transfers between devices, exchange(): corners = [lax.ppermute(x, axes, p) for x, p in zip(near, pairs)]  6.44 us
    ppermute x2, starting transfers between devices, exchange(): lax.ppermute(pack, 'gx', [((g + 1) % across, g) for g in range(across)])  4.98 us
    ppermute x4, waiting for transfers between devices, exchange(): corners = [lax.ppermute(x, axes, p) for x, p in zip(near, pairs)]  4.73 us
    ppermute x2, waiting for transfers between devices, exchange(): lax.ppermute(pack, 'gx', [((g + 1) % across, g) for g in range(across)])  3.92 us
    ppermute x2, starting transfers between devices, exchange(): lax.ppermute(pack, 'gx', [(g, (g + 1) % across) for g in range(across)])  1.47 us
  transfers between devices with their start and end apart: 12, of which 5 were waited for; matrix products, arithmetic and copies ran while one was open for 0% of the time, Pallas kernels for 3%

commit v1 on v0

--- a/solution.py
+++ b/solution.py
@@ -21,9 +21,9 @@
 PAIRS = [(i, j) for i in range(NV) for j in range(i, NV)]
 EARLY = [(i, j) for i, j in PAIRS if j < 5]
 PEERS = 256
+ROWS = F * T * R
 SIDE = 2 * TP
 FLOW = 208
-VM = pl.BlockSpec(memory_space=pltpu.VMEM)
 
 
 def time_matrices():
@@ -180,7 +180,7 @@
     ]
 
 
-def steps(mats, exts, slabs, flow, sflow, td, std, merged, basis, first):
+def steps(mats, exts, slabs, flow, sflow, td, std, merged, outs):
     north, south, _, _ = masks()
     side_ok = side_masks((8, 128))
     lane = lanes((8, 128))
@@ -245,7 +245,7 @@
                     side_new[f, p, s] = out[f] * side_ok[p]
         for f in range(F):
             for r in range(R):
-                basis[first + k, f * R + r] = dst[f, H + r]
+                outs[k][pl.ds(f * T * R + r, T, stride=R), :] = dst[f, H + r, 0:T]
 
 
 def by_parity(load, *pairs):
@@ -258,7 +258,7 @@
         load(*[pair[1] for pair in pairs], *[pair[0] for pair in pairs])
 
 
-def first_kernel(own, even, odd, here, near_even, near_odd, mats, main, pack, basis, flow, sflow, ext0, ext1, side0, side1, td, std, merged):
+def first_kernel(own, even, odd, here, near_even, near_odd, mats, main, pack, older, flow, sflow, ext0, ext1, side0, side1, td, std, merged):
     half = 0.5 * STEP
 
     def load(north, flow_north, south, flow_south):
@@ -287,52 +287,56 @@
                 sflow[j, p] = sflow[j, p] * jnp.where(halo, scale, 1.0)
 
     by_parity(load, (even, odd), (near_even, near_odd))
-    for f in range(F):
-        for r in range(R):
-            basis[0, f * R + r] = ext0[f, H + r]
-    steps(mats, (ext0, ext1), (side0, side1), flow, sflow, td, std, merged, basis, 1)
-    for f in range(F):
-        for r in range(R):
-            main[pl.ds(f * T * R + r, T, stride=R), :] = basis[H, f * R + r, 0:T]
+    older[0] = own[0:ROWS, :]
+    outs = [older.at[k] for k in (1, 2, 3)] + [main]
+    steps(mats, (ext0, ext1), (side0, side1), flow, sflow, td, std, merged, outs)
     for g in range(2):
         total = jnp.zeros((TP, 128), jnp.float32)
         for j in range(4 if g == 0 else 2):
             for r in range(R):
-                total = total + window(basis[H, (g * 4 + j) * R + r], j * 32 + r * 8)
+                total = total + window(ext0[g * 4 + j, H + r], j * 32 + r * 8)
         pack[g * TP : (g + 1) * TP, :] = total
 
 
-def products(slabs, pairs):
-    def slab(i, sums):
+def products(vectors, pairs):
+    def part(i, sums):
         sums = list(sums)
-        for c in range(TP // 8):
-            s = pl.ds(8 * c, 8)
-            vec = [get(i, s) for get in slabs]
+        for c in range(9):
+            s = pl.ds(pl.multiple_of(72 * i, 8) + 8 * c, 8)
+            vec = {k: get(s) for k, get in vectors.items()}
             for e, (a, b) in enumerate(pairs):
                 sums[e] = sums[e] + vec[a] * vec[b]
         return tuple(sums)
 
     zero = jnp.zeros((8, 128), jnp.float32)
-    return lax.fori_loop(0, F * R, slab, (zero,) * len(pairs), unroll=2)
-
-
-def gram_kernel(older, early):
-    slabs = [lambda i, s, k=k: older[k, i, s] for k in range(5)]
-    for e, value in enumerate(products(slabs, EARLY)):
+    return lax.fori_loop(0, ROWS // 72, part, (zero,) * len(pairs))
+
+
+def early_vectors(older, main):
+    vectors = {k: lambda s, k=k: older[k, s] for k in range(H)}
+    vectors[H] = lambda s: main[s]
+    return vectors
+
+
+def gram_kernel(older, main, early):
+    for e, value in enumerate(products(early_vectors(older, main), EARLY)):
         early[e] = value
 
 
-def second_kernel(own, even, odd, here, corner_even, corner_odd, flow, sflow, older, early, mats, basis, gram, ext0, ext1, side0, side1, td, std, merged, rows):
+def second_kernel(own, even, odd, here, corner_even, corner_odd, flow, sflow, older, early, mats, newer, gram, ext0, ext1, side0, side1, td, std, merged, rows):
 
     def load(north, above, south, below):
         fill(own, north, south, [slabs_of(ref) for ref in (above, here, below)], ext0, side0)
 
     by_parity(load, (even, odd), (corner_even, corner_odd))
-    steps(mats, (ext0, ext1), (side0, side1), flow, sflow, td, std, merged, basis, 0)
+    outs = [newer.at[k] for k in range(4)]
+    steps(mats, (ext0, ext1), (side0, side1), flow, sflow, td, std, merged, outs)
 
     late = [pair for pair in PAIRS if pair not in EARLY]
-    slabs = [lambda i, s, k=k: older[k, i, s] for k in range(5)] + [lambda i, s, k=k: basis[k, i, s] for k in range(4)]
-    sums = dict(zip(late, products(slabs, late)))
+    vectors = early_vectors(older, own)
+    for k in range(4):
+        vectors[5 + k] = lambda s, k=k: newer[k, s]
+    sums = dict(zip(late, products(vectors, late)))
     for e, pair in enumerate(EARLY):
         sums[pair] = early[e]
     rows[...] = jnp.zeros((48, 128), jnp.float32)
@@ -399,7 +403,7 @@
     return step, rest
 
 
-def last_kernel(parts, older, newer, solution, residual):
+def last_kernel(parts, older, main, newer, solution, residual, sol, res, sems):
     total = jnp.sum(parts[...].reshape(PEERS // 8, 8, 128), axis=0)
     total = jnp.sum(total, axis=0, keepdims=True)
     gram = [[None] * NV for _ in range(NV)]
@@ -410,36 +414,46 @@
     rest = [zero if a is None else a for a in rest]
     step2, rest = cycle(gram, rest)
     step = [plus(a, b) for a, b in zip(step1, step2)]
-    step = [None if a is None else a[0:1] for a in step]
-    rest = [a[0:1] for a in rest]
-
-    def slab(i, carry):
-        f, r = i // R, i % R
-        sol = res = None
-        for k in range(NV):
-            x = older[k, i, 0:T] if k < 5 else newer[k - 5, i, 0:T]
-            if step[k] is not None:
-                sol = plus(sol, step[k] * x)
-            res = plus(res, rest[k] * x)
-        solution[pl.ds(f * T * R + r, T, stride=R), :] = sol
-        residual[pl.ds(f * T * R + r, T, stride=R), :] = res
-        return carry
-
-    lax.fori_loop(0, F * R, slab, 0)
+    vectors = early_vectors(older, main)
+    for k in range(4):
+        vectors[5 + k] = lambda s, k=k: newer[k, s]
+    copies = []
+    third = ROWS // 3
+    for p in range(3):
+
+        def part(i, carry, p=p):
+            for c in range(11):
+                s = pl.ds(pl.multiple_of(p * third + 88 * i, 8) + 8 * c, 8)
+                one = two = None
+                for k in range(NV):
+                    x = vectors[k](s)
+                    one = plus(one, times(step[k], x))
+                    two = plus(two, rest[k] * x)
+                sol[s, :] = one
+                res[s, :] = two
+            return carry
+
+        lax.fori_loop(0, third // 88, part, 0)
+        for n, (src, dst) in enumerate(((sol, solution), (res, residual))):
+            s = pl.ds(p * third, third)
+            copies.append(pltpu.make_async_copy(src.at[s], dst.at[s], sems.at[2 * p + n]))
+            copies[-1].start()
+    for copy in copies:
+        copy.wait()
 
 
 def call(kernel, args, outs, scratch=(), first=False, final=False):
     space = pltpu.HBM if first else pltpu.VMEM
     args = [pltpu.with_memory_space_constraint(a, space) for a in args]
-    make = jax.ShapeDtypeStruct if final else pltpu.VMEM
+    make = pltpu.HBM if final else pltpu.VMEM
     kinds = [jnp.bfloat16 if shape[-1] == 2 * TP else jnp.float32 for shape in outs]
     scratch = [pltpu.VMEM(shape, jnp.float32) for shape in scratch]
     return pl.pallas_call(
         kernel,
         out_shape=[make(shape, kind) for shape, kind in zip(outs, kinds)],
         in_specs=[pl.BlockSpec(memory_space=space)] * len(args),
-        out_specs=[VM] * len(outs),
-        scratch_shapes=scratch + [pltpu.SemaphoreType.DMA((4,))] * first,
+        out_specs=[pl.BlockSpec(memory_space=make)] * len(outs),
+        scratch_shapes=scratch + [pltpu.SemaphoreType.DMA((6,))] * (first or final),
         compiler_params=pltpu.CompilerParams(vmem_limit_bytes=24 << 20),
     )(*args)
 
@@ -489,24 +503,25 @@
         ((8 * T * R + 8, 128), (SIDE + FLOW, 128), (SIDE + FLOW, 128), (SIDE, 128), (2, 2 * TP, 2 * TP)),
         first=True,
     )
-    own, pack, older, flows, side_flows = call(
+    main, pack, older, flows, side_flows = call(
         first_kernel,
         (own, *exchange(rs, pack, (to_even, to_odd)), mats),
-        ((F * T * R, 128), (2 * TP, 128), (5, F * R, TP, 128), (2, E, TP, 128), (2, 2, TP, 128)),
+        ((ROWS, 128), (SIDE, 128), (H, ROWS, 128), (2, E, TP, 128), (2, 2, TP, 128)),
         WORK,
     )
-    (early,) = call(gram_kernel, (older,), ((len(EARLY), 8, 128),))
+    (early,) = call(gram_kernel, (older, main), ((len(EARLY), 8, 128),))
     newer, gram = call(
         second_kernel,
-        (own, *exchange(own, pack), flows, side_flows, older, early, mats),
-        ((4, F * R, TP, 128), (PEERS, 128)),
+        (main, *exchange(main, pack), flows, side_flows, older, early, mats),
+        ((4, ROWS, 128), (PEERS, 128)),
         WORK + ((48, 128),),
     )
     parts = lax.all_to_all(gram.reshape(PEERS, 1, 128), ("gx", "gy"), 0, 0, tiled=True)
     solution_field, residual = call(
         last_kernel,
-        (parts.reshape(PEERS, 128), older, newer),
-        ((F * T * R, 128), (F * T * R, 128)),
+        (parts.reshape(PEERS, 128), older, main, newer),
+        ((ROWS, 128), (ROWS, 128)),
+        ((ROWS, 128), (ROWS, 128)),
         final=True,
     )
     return solution_field.reshape(right_side.shape), residual.reshape(right_side.shape)

time: 72.2 us -> 71.8 us (level)
  transfers between devices with their start and end apart: 12 -> 12, of which waited for: 5 -> 5; matrix products, arithmetic and copies ran while one was open for 0% -> 0% of each run, Pallas kernels for 3% -> 2%
where the time goes in v1:
time: 71.8 us; the launch traced here: 71.7 us
  blocking collectives  26.1 us (36%)
  starting transfers between devices  21.1 us (29%)
  Pallas kernels  14.9 us (21%)
  waiting for transfers between devices  8.75 us (12%)
  between operations  0.85 us (1%)
    all_to_all x1, blocking collectives, shards(): lax.all_to_all(gram.reshape(PEERS, 1, 128), ('gx', 'gy'), 0, 0, tiled=True)  26.1 us
    pallas_call x5, Pallas kernels, call(): pl.pallas_call(kernel, out_shape=[make(shape, kind) for shape, kind in zi...  14.9 us
    ppermute x4, starting transfers between devices, exchange(): rows = [lax.ppermute(rows, axes, p) for p in pairs]  8.18 us
    ppermute x4, starting transfers between devices, exchange(): corners = [lax.ppermute(x, axes, p) for x, p in zip(near, pairs)]  6.44 us
    ppermute x2, starting transfers between devices, exchange(): lax.ppermute(pack, 'gx', [((g + 1) % across, g) for g in range(across)])  5.01 us
    ppermute x4, waiting for transfers between devices, exchange(): corners = [lax.ppermute(x, axes, p) for x, p in zip(near, pairs)]  4.81 us
    ppermute x2, waiting for transfers between devices, exchange(): lax.ppermute(pack, 'gx', [((g + 1) % across, g) for g in range(across)])  3.92 us
    ppermute x2, starting transfers between devices, exchange(): lax.ppermute(pack, 'gx', [(g, (g + 1) % across) for g in range(across)])  1.46 us
  transfers between devices with their start and end apart: 12, of which 5 were waited for; matrix products, arithmetic and copies ran while one was open for 0% of the time, Pallas kernels for 2%

profile of v1, /device:TPU:1, one launch (start us, length us, event | category | flops | bytes accessed | tf_op | source)
XLA Modules:
  0.0 71.7 jit_solution(18092300520771217037)
XLA Ops:
  0.6 3.3 %collective-permute-start.1 = (f32[792,128]{1,0:T(8,128)}, f32[792,128]{1,0:T(8,128)S(1)}, u32[]{:S(2)}, u32[]{:S(2)}) collective-permute-start(f32[792,128]{1,0:T(8,128)} %bitcast.10), channel_id=1, source_target_pairs={{0,32},{1,2},{2,1},{3,4},{4,3},{5,6},{6,5},{7,8},{8,7},{9,10},{10,... | collective-permute-start | bytes 1216520 | tf_op jit(solution)/shard_map/ppermute | solution.py:476
  4.0 0.9 %collective-permute-start = (f32[792,128]{1,0:T(8,128)}, f32[792,128]{1,0:T(8,128)S(1)}, u32[]{:S(2)}, u32[]{:S(2)}) collective-permute-start(f32[792,128]{1,0:T(8,128)} %bitcast.11), channel_id=1, source_target_pairs={{0,1},{1,0},{2,3},{3,2},{4,5},{5,4},{6,7},{7,6},{8,9},{9,8},{10,11... | collective-permute-start | bytes 1216520 | tf_op jit(solution)/shard_map/ppermute | solution.py:476
  4.8 1.4 %shard_map.59 = (f32[1064,128]{1,0:T(8,128)S(1)}, f32[288,128]{1,0:T(8,128)S(1)}, f32[288,128]{1,0:T(8,128)S(1)}, f32[80,128]{1,0:T(8,128)S(1)}, bf16[2,80,80]{2,1,0:T(8,128)(2,1)S(1)}) custom-call(f32[792,128]{1,0:T(8,128)} %bitcast.12, f32[264,128]{1,0:T(8,128)} %bitcast.13, f32[4,128]{1,0:T(4,128)} %relax.1, bf16[2,80,80]{2,1,0:T(8,128)(2,1)} %constant.70.clone.mats_in), custom_call_target="tpu_custom_call" | custom-call | tf_op jit(solution)/shard_map/pallas_call | solution.py:451
  6.2 1.2 %collective-permute-start.3 = (f32[80,128]{1,0:T(8,128)S(1)}, f32[80,128]{1,0:T(8,128)S(1)}, u32[]{:S(2)}, u32[]{:S(2)}) collective-permute-start(f32[80,128]{1,0:T(8,128)S(1)} %get-tuple-element.41), channel_id=1, source_target_pairs={{32,0},{64,32},{96,64},{128,96},{160,128},{192,160},{224,192},{0,2... | collective-permute-start | bytes 122888 | tf_op jit(solution)/shard_map/ppermute | solution.py:478
  7.4 1.2 %collective-permute-start.2 = (f32[80,128]{1,0:T(8,128)S(1)}, f32[80,128]{1,0:T(8,128)S(1)}, u32[]{:S(2)}, u32[]{:S(2)}) collective-permute-start(f32[80,128]{1,0:T(8,128)S(1)} %get-tuple-element.41), channel_id=1, source_target_pairs={{0,32},{32,64},{64,96},{96,128},{128,160},{160,192},{192,224},{224... | collective-permute-start | bytes 122888 | tf_op jit(solution)/shard_map/ppermute | solution.py:477
  8.6 1.9 %collective-permute-done.3 = f32[80,128]{1,0:T(8,128)S(1)} collective-permute-done((f32[80,128]{1,0:T(8,128)S(1)}, f32[80,128]{1,0:T(8,128)S(1)}, u32[]{:S(2)}, u32[]{:S(2)}) %collective-permute-start.3) | collective-permute-done | bytes 40992 | tf_op jit(solution)/shard_map/ppermute | solution.py:478
  10.6 0.0 collective-permute-done.2
  10.6 0.1 collective-permute-start.4
  10.7 3.6 %collective-permute-start.5 = (f32[288,128]{1,0:T(8,128)S(1)}, f32[288,128]{1,0:T(8,128)S(1)}, u32[]{:S(2)}, u32[]{:S(2)}) collective-permute-start(f32[288,128]{1,0:T(8,128)S(1)} %get-tuple-element.54), channel_id=1, source_target_pairs={{0,32},{1,2},{2,1},{3,4},{4,3},{5,6},{6,5},{7,8},{8,7},{9,10},{10,... | collective-permute-start | bytes 442376 | tf_op jit(solution)/shard_map/ppermute | solution.py:482
  14.4 2.5 %collective-permute-done.4.near_even = f32[288,128]{1,0:T(8,128)S(1)} collective-permute-done((f32[288,128]{1,0:T(8,128)S(1)}, f32[288,128]{1,0:T(8,128)S(1)}, u32[]{:S(2)}, u32[]{:S(2)}) %collective-permute-start.4) | collective-permute-done | bytes 147488 | tf_op jit(solution)/shard_map/ppermute | solution.py:482
  16.9 5.3 %shard_map.60 = (f32[792,128]{1,0:T(8,128)S(1)}, f32[80,128]{1,0:T(8,128)S(1)}, f32[4,792,128]{2,1,0:T(8,128)S(1)}, f32[2,12,40,128]{3,2,1,0:T(8,128)S(1)}, f32[2,2,40,128]{3,2,1,0:T(8,128)S(1)}) custom-call(f32[1064,128]{1,0:T(8,128)S(1)} %get-tuple-element.40.own, f32[792,128]{1,0:T(8,128)S(1)} %collective-permute-done.even, ...), custom_call_target="tpu_custom_call" | custom-call | tf_op jit(solution)/shard_map/pallas_call | solution.py:451
  22.2 2.4 %collective-permute-start.7 = (f32[792,128]{1,0:T(8,128)S(1)}, f32[792,128]{1,0:T(8,128)S(1)}, u32[]{:S(2)}, u32[]{:S(2)}) collective-permute-start(f32[792,128]{1,0:T(8,128)S(1)} %get-tuple-element.45.main.own), channel_id=1, source_target_pairs={{0,32},{1,2},{2,1},{3,4},{4,3},{5,6},{6,5},{7,8},{8,7},{9,10},{10,... | collective-permute-start | bytes 1216520 | tf_op jit(solution)/shard_map/ppermute | solution.py:476
  24.7 1.6 %collective-permute-start.6 = (f32[792,128]{1,0:T(8,128)S(1)}, f32[792,128]{1,0:T(8,128)S(1)}, u32[]{:S(2)}, u32[]{:S(2)}) collective-permute-start(f32[792,128]{1,0:T(8,128)S(1)} %get-tuple-element.45.main.own), channel_id=1, source_target_pairs={{0,1},{1,0},{2,3},{3,2},{4,5},{5,4},{6,7},{7,6},{8,9},{9,8},{10,11... | collective-permute-start | bytes 1216520 | tf_op jit(solution)/shard_map/ppermute | solution.py:476
  26.2 3.8 %collective-permute-start.9 = (f32[80,128]{1,0:T(8,128)S(1)}, f32[80,128]{1,0:T(8,128)S(1)}, u32[]{:S(2)}, u32[]{:S(2)}) collective-permute-start(f32[80,128]{1,0:T(8,128)S(1)} %get-tuple-element.46), channel_id=1, source_target_pairs={{32,0},{64,32},{96,64},{128,96},{160,128},{192,160},{224,192},{0,2... | collective-permute-start | bytes 122888 | tf_op jit(solution)/shard_map/ppermute | solution.py:478
  30.0 0.3 collective-permute-start.8
  30.2 2.0 %collective-permute-done.9 = f32[80,128]{1,0:T(8,128)S(1)} collective-permute-done((f32[80,128]{1,0:T(8,128)S(1)}, f32[80,128]{1,0:T(8,128)S(1)}, u32[]{:S(2)}, u32[]{:S(2)}) %collective-permute-start.9) | collective-permute-done | bytes 40992 | tf_op jit(solution)/shard_map/ppermute | solution.py:478
  32.2 2.6 %collective-permute-start.11 = (f32[80,128]{1,0:T(8,128)S(1)}, f32[80,128]{1,0:T(8,128)S(1)}, u32[]{:S(2)}, u32[]{:S(2)}) collective-permute-start(f32[80,128]{1,0:T(8,128)S(1)} %fusion.here), channel_id=1, source_target_pairs={{0,32},{1,2},{2,1},{3,4},{4,3},{5,6},{6,5},{7,8},{8,7},{9,10},{10,... | collective-permute-start | bytes 122888 | tf_op jit(solution)/shard_map/ppermute | solution.py:482
  34.8 0.1 collective-permute-start.10
  34.9 0.4 shard_map.61.early
  35.3 0.3 collective-permute-done.11.corner_odd
  35.7 2.0 %collective-permute-done.10.corner_even = f32[80,128]{1,0:T(8,128)S(1)} collective-permute-done((f32[80,128]{1,0:T(8,128)S(1)}, f32[80,128]{1,0:T(8,128)S(1)}, u32[]{:S(2)}, u32[]{:S(2)}) %collective-permute-start.10) | collective-permute-done | bytes 40992 | tf_op jit(solution)/shard_map/ppermute | solution.py:482
  37.7 6.2 %shard_map.62 = (f32[4,792,128]{2,1,0:T(8,128)S(1)}, f32[256,128]{1,0:T(8,128)S(1)}) custom-call(f32[792,128]{1,0:T(8,128)S(1)} %get-tuple-element.45.main.own, f32[792,128]{1,0:T(8,128)S(1)} %collective-permute-done.6.even, f32[792,128]{1,0:T(8,128)S(1)} %collective-permute-done.7.odd, f32[80,128]{1,0:T(8,128)S(1)} %fusion.here, ...), custom_call_target="tpu_custom_call" | custom-call | tf_op jit(solution)/shard_map/pallas_call | solution.py:451
  43.9 26.1 %all_to_all.5 = f32[256,1,128]{2,1,0:T(1,128)S(1)} all-to-all(f32[256,1,128]{2,1,0:T(1,128)S(1)} %bitcast.9), channel_id=1, replica_groups=mesh['gx'=8,'gy'=32] {'gx','gy'}, dimensions={0} | all-to-all | bytes 262144 | tf_op jit(solution)/shard_map/all_to_all | solution.py:519
  70.0 1.6 %shard_map.63 = (f32[792,128]{1,0:T(8,128)}, f32[792,128]{1,0:T(8,128)}) custom-call(f32[256,128]{1,0:T(8,128)S(1)} %bitcast.8, f32[4,792,128]{2,1,0:T(8,128)S(1)} %get-tuple-element.49.older, f32[792,128]{1,0:T(8,128)S(1)} %get-tuple-element.45.main.own, f32[4,792,128]{2,1,0:T(8,128)S(1)} %get-tuple-element.51.newer), custom_call_target="tpu_custom_call" | custom-call | tf_op jit(solution)/shard_map/pallas_call | solution.py:451
  (11 shorter events, 0.0 us)
Async XLA Ops:
  0.6 16.2 %collective-permute-start.1 = (f32[792,128]{1,0:T(8,128)}, f32[792,128]{1,0:T(8,128)S(1)}, u32[]{:S(2)}, u32[]{:S(2)}) collective-permute-start(f32[792,128]{1,0:T(8,128)} %bitcast.10), channel_id=1, source_target_pairs={{0,32},{1,2},{2,1},{3,4},{4,3},{5,6},{6,5},{7,8},{8,7},{9,10},{10,... | collective-permute-start | bytes 1216520 | tf_op jit(solution)/shard_map/ppermute | solution.py:476
  4.0 12.9 %collective-permute-start = (f32[792,128]{1,0:T(8,128)}, f32[792,128]{1,0:T(8,128)S(1)}, u32[]{:S(2)}, u32[]{:S(2)}) collective-permute-start(f32[792,128]{1,0:T(8,128)} %bitcast.11), channel_id=1, source_target_pairs={{0,1},{1,0},{2,3},{3,2},{4,5},{5,4},{6,7},{7,6},{8,9},{9,8},{10,11... | collective-permute-start | bytes 1216520 | tf_op jit(solution)/shard_map/ppermute | solution.py:476
  6.2 4.4 %collective-permute-start.3 = (f32[80,128]{1,0:T(8,128)S(1)}, f32[80,128]{1,0:T(8,128)S(1)}, u32[]{:S(2)}, u32[]{:S(2)}) collective-permute-start(f32[80,128]{1,0:T(8,128)S(1)} %get-tuple-element.41), channel_id=1, source_target_pairs={{32,0},{64,32},{96,64},{128,96},{160,128},{192,160},{224,192},{0,2... | collective-permute-start | bytes 122888 | tf_op jit(solution)/shard_map/ppermute | solution.py:478
  7.4 3.2 %collective-permute-start.2 = (f32[80,128]{1,0:T(8,128)S(1)}, f32[80,128]{1,0:T(8,128)S(1)}, u32[]{:S(2)}, u32[]{:S(2)}) collective-permute-start(f32[80,128]{1,0:T(8,128)S(1)} %get-tuple-element.41), channel_id=1, source_target_pairs={{0,32},{32,64},{64,96},{96,128},{128,160},{160,192},{192,224},{224... | collective-permute-start | bytes 122888 | tf_op jit(solution)/shard_map/ppermute | solution.py:477
  10.6 6.2 %collective-permute-start.4 = (f32[288,128]{1,0:T(8,128)S(1)}, f32[288,128]{1,0:T(8,128)S(1)}, u32[]{:S(2)}, u32[]{:S(2)}) collective-permute-start(f32[288,128]{1,0:T(8,128)S(1)} %constant_dynamic-update-slice_fusion.1), channel_id=1, source_target_pairs={{0,1},{1,0},{2,3},{3,2},{4,5},{5,4},{6,7},{7,6},{8,9},{9,8},{10,11... | collective-permute-start | bytes 442376 | tf_op jit(solution)/shard_map/ppermute | solution.py:482
  10.7 6.1 %collective-permute-start.5 = (f32[288,128]{1,0:T(8,128)S(1)}, f32[288,128]{1,0:T(8,128)S(1)}, u32[]{:S(2)}, u32[]{:S(2)}) collective-permute-start(f32[288,128]{1,0:T(8,128)S(1)} %get-tuple-element.54), channel_id=1, source_target_pairs={{0,32},{1,2},{2,1},{3,4},{4,3},{5,6},{6,5},{7,8},{8,7},{9,10},{10,... | collective-permute-start | bytes 442376 | tf_op jit(solution)/shard_map/ppermute | solution.py:482
  22.2 15.4 %collective-permute-start.7 = (f32[792,128]{1,0:T(8,128)S(1)}, f32[792,128]{1,0:T(8,128)S(1)}, u32[]{:S(2)}, u32[]{:S(2)}) collective-permute-start(f32[792,128]{1,0:T(8,128)S(1)} %get-tuple-element.45.main.own), channel_id=1, source_target_pairs={{0,32},{1,2},{2,1},{3,4},{4,3},{5,6},{6,5},{7,8},{8,7},{9,10},{10,... | collective-permute-start | bytes 1216520 | tf_op jit(solution)/shard_map/ppermute | solution.py:476
  24.7 13.0 %collective-permute-start.6 = (f32[792,128]{1,0:T(8,128)S(1)}, f32[792,128]{1,0:T(8,128)S(1)}, u32[]{:S(2)}, u32[]{:S(2)}) collective-permute-start(f32[792,128]{1,0:T(8,128)S(1)} %get-tuple-element.45.main.own), channel_id=1, source_target_pairs={{0,1},{1,0},{2,3},{3,2},{4,5},{5,4},{6,7},{7,6},{8,9},{9,8},{10,11... | collective-permute-start | bytes 1216520 | tf_op jit(solution)/shard_map/ppermute | solution.py:476
  26.2 6.0 %collective-permute-start.9 = (f32[80,128]{1,0:T(8,128)S(1)}, f32[80,128]{1,0:T(8,128)S(1)}, u32[]{:S(2)}, u32[]{:S(2)}) collective-permute-start(f32[80,128]{1,0:T(8,128)S(1)} %get-tuple-element.46), channel_id=1, source_target_pairs={{32,0},{64,32},{96,64},{128,96},{160,128},{192,160},{224,192},{0,2... | collective-permute-start | bytes 122888 | tf_op jit(solution)/shard_map/ppermute | solution.py:478
  30.0 2.2 %collective-permute-start.8 = (f32[80,128]{1,0:T(8,128)S(1)}, f32[80,128]{1,0:T(8,128)S(1)}, u32[]{:S(2)}, u32[]{:S(2)}) collective-permute-start(f32[80,128]{1,0:T(8,128)S(1)} %get-tuple-element.46), channel_id=1, source_target_pairs={{0,32},{32,64},{64,96},{96,128},{128,160},{160,192},{192,224},{224... | collective-permute-start | bytes 122888 | tf_op jit(solution)/shard_map/ppermute | solution.py:477
  32.2 3.5 %collective-permute-start.11 = (f32[80,128]{1,0:T(8,128)S(1)}, f32[80,128]{1,0:T(8,128)S(1)}, u32[]{:S(2)}, u32[]{:S(2)}) collective-permute-start(f32[80,128]{1,0:T(8,128)S(1)} %fusion.here), channel_id=1, source_target_pairs={{0,32},{1,2},{2,1},{3,4},{4,3},{5,6},{6,5},{7,8},{8,7},{9,10},{10,... | collective-permute-start | bytes 122888 | tf_op jit(solution)/shard_map/ppermute | solution.py:482
  34.8 2.9 %collective-permute-start.10 = (f32[80,128]{1,0:T(8,128)S(1)}, f32[80,128]{1,0:T(8,128)S(1)}, u32[]{:S(2)}, u32[]{:S(2)}) collective-permute-start(f32[80,128]{1,0:T(8,128)S(1)} %fusion.here), channel_id=1, source_target_pairs={{0,1},{1,0},{2,3},{3,2},{4,5},{5,4},{6,7},{7,6},{8,9},{9,8},{10,11... | collective-permute-start | bytes 122888 | tf_op jit(solution)/shard_map/ppermute | solution.py:482

commit v2 on v1

--- a/solution.py
+++ b/solution.py
@@ -128,14 +128,17 @@
     dst[f, 1] = jnp.where(slot < 4, own, halo) * ok[1]
 
 
-def own_windows(slab, rows=range(E)):
-    total = jnp.zeros((TP, 128), jnp.float32)
-    for e in rows:
-        total = total + window(slab(e), e * 8)
+def own_windows(slab, pack, f, scale=None):
+    lane = lanes()
+    here = pltpu.roll(pack[pl.ds(f // 4 * TP, TP)], (8 * H - 32 * (f % 4)) % 128, 1)
+    total = jnp.where((lane >= 8 * H) & (lane < 8 * (H + R)), here if scale is None else here * scale, 0.0)
+    for e in range(1, E - 1):
+        if not H <= e < H + R:
+            total = total + window(slab(e), e * 8)
     return total
 
 
-def fill(own, north, south, sides, ext, side):
+def fill(own, pack, north, south, sides, ext, side):
     ok_north, ok_south, _, _ = masks()
     ok = side_masks((1, 128))
     for f in range(F):
@@ -144,7 +147,7 @@
             put(ext, (f, H + r), raw(own, f, r))
             put(ext, (f, H + R + r), raw(south, f, r), ok_south)
     for f in range(F):
-        sides_of(side, f, own_windows(lambda e: ext[f, e]), sides, f // 4, f % 4, ok)
+        sides_of(side, f, own_windows(lambda e: ext[f, e], pack, f), sides, f // 4, f % 4, ok)
 
 
 def masks():
@@ -204,7 +207,6 @@
                 td[n, r], td[n, r + 1] = timed(f, src[f, r], src[f, r + 1])
 
         def main_pair(r, src=src, dst=dst):
-            keep = [jnp.where(e < H, north, jnp.where(e < H + R, jnp.float32(1.0), south)) for e in (r, r + 1)]
             for c in range(TP // 8):
                 s = pl.ds(8 * c, 8)
                 rows = [[src[f, r + e, s] for f in range(F)] for e in (-1, 0, 1, 2)]
@@ -218,13 +220,8 @@
                     times = {f: td[n, r + e, s] for n, f in enumerate(TIMED)}
                     out = combine(core, xm, xp, ym, yp, flow[0, r + e, s], flow[1, r + e, s], rl, times)
                     for f in range(F):
-                        dst[f, r + e, s] = out[f] * keep[e]
-
-        def pair(i, carry, low=low, time_pair=time_pair, main_pair=main_pair):
-            r = low + 2 * i
-            time_pair(jnp.minimum(r + 2, E - 2))
-            main_pair(r)
-            return carry
+                        inside = H <= r + e < H + R
+                        dst[f, r + e, s] = out[f] if inside else out[f] * (north if r + e < H else south)
 
         for f in range(F):
             merged[f] = jnp.where(lanes() % 8 == 3, side[f, 0], pltpu.roll(side[f, 1], 126, 1))
@@ -232,7 +229,10 @@
             for n, f in enumerate(TIMED):
                 std[n, 0], std[n, 1] = timed(f, side[f, 0], side[f, 1])
         time_pair(low)
-        lax.fori_loop(0, count // 2, pair, 0, unroll=True)
+        for i in range(count // 2):
+            if i + 1 < count // 2:
+                time_pair(low + 2 * i + 2)
+            main_pair(low + 2 * i)
         for p in range(0 if last else 2):
             for c in range(TP // 8):
                 s = pl.ds(8 * c, 8)
@@ -258,12 +258,12 @@
         load(*[pair[1] for pair in pairs], *[pair[0] for pair in pairs])
 
 
-def first_kernel(own, even, odd, here, near_even, near_odd, mats, main, pack, older, flow, sflow, ext0, ext1, side0, side1, td, std, merged):
+def first_kernel(own, own_pack, even, odd, here, near_even, near_odd, mats, main, pack, older, flow, sflow, ext0, ext1, side0, side1, td, std, merged):
     half = 0.5 * STEP
 
     def load(north, flow_north, south, flow_south):
         sides = [slabs_of(ref) for ref in (flow_north, here, flow_south)]
-        fill(own, north, south, sides, ext0, side0)
+        fill(own, own_pack, north, south, sides, ext0, side0)
         for j in range(2):
             for r in range(R):
                 put(flow, (j, H + r), raw(own, F + j, r), half)
@@ -281,7 +281,7 @@
         scale = jnp.where(sub == T, STEP, half).astype(jnp.float32)
         slot = lanes() % 8
         for j in range(2):
-            sides_of(sflow, j, own_windows(lambda e: flow[j, e], range(1, E - 1)), sides, 1, 2 + j, (1.0, 1.0))
+            sides_of(sflow, j, own_windows(lambda e: flow[j, e], own_pack, F + j, scale), sides, 1, 2 + j, (1.0, 1.0))
             for p in range(2):
                 halo = (slot < 4) if p == 0 else (slot >= 4)
                 sflow[j, p] = sflow[j, p] * jnp.where(halo, scale, 1.0)
@@ -323,10 +323,10 @@
         early[e] = value
 
 
-def second_kernel(own, even, odd, here, corner_even, corner_odd, flow, sflow, older, early, mats, newer, gram, ext0, ext1, side0, side1, td, std, merged, rows):
+def second_kernel(own, own_pack, even, odd, here, corner_even, corner_odd, flow, sflow, older, early, mats, newer, gram, ext0, ext1, side0, side1, td, std, merged, rows):
 
     def load(north, above, south, below):
-        fill(own, north, south, [slabs_of(ref) for ref in (above, here, below)], ext0, side0)
+        fill(own, own_pack, north, south, [slabs_of(ref) for ref in (above, here, below)], ext0, side0)
 
     by_parity(load, (even, odd), (corner_even, corner_odd))
     outs = [newer.at[k] for k in range(4)]
@@ -505,14 +505,14 @@
     )
     main, pack, older, flows, side_flows = call(
         first_kernel,
-        (own, *exchange(rs, pack, (to_even, to_odd)), mats),
+        (own, pack, *exchange(rs, pack, (to_even, to_odd)), mats),
         ((ROWS, 128), (SIDE, 128), (H, ROWS, 128), (2, E, TP, 128), (2, 2, TP, 128)),
         WORK,
     )
     (early,) = call(gram_kernel, (older, main), ((len(EARLY), 8, 128),))
     newer, gram = call(
         second_kernel,
-        (main, *exchange(main, pack), flows, side_flows, older, early, mats),
+        (main, pack, *exchange(main, pack), flows, side_flows, older, early, mats),
         ((4, ROWS, 128), (PEERS, 128)),
         WORK + ((48, 128),),
     )

time: 71.8 us -> 71.3 us (level)
  transfers between devices with their start and end apart: 12 -> 12, of which waited for: 5 -> 5; matrix products, arithmetic and copies ran while one was open for 0% -> 0% of each run, Pallas kernels for 2% -> 3%
where the time goes in v2:
time: 71.3 us; the launch traced here: 71.1 us
  blocking collectives  26.1 us (37%)
  starting transfers between devices  21.1 us (30%)
  Pallas kernels  14.3 us (20%)
  waiting for transfers between devices  8.74 us (12%)
  between operations  0.85 us (1%)
    all_to_all x1, blocking collectives, shards(): lax.all_to_all(gram.reshape(PEERS, 1, 128), ('gx', 'gy'), 0, 0, tiled=True)  26.1 us
    pallas_call x5, Pallas kernels, call(): pl.pallas_call(kernel, out_shape=[make(shape, kind) for shape, kind in zi...  14.3 us
    ppermute x4, starting transfers between devices, exchange(): rows = [lax.ppermute(rows, axes, p) for p in pairs]  8.18 us
    ppermute x4, starting transfers between devices, exchange(): corners = [lax.ppermute(x, axes, p) for x, p in zip(near, pairs)]  6.44 us
    ppermute x2, starting transfers between devices, exchange(): lax.ppermute(pack, 'gx', [((g + 1) % across, g) for g in range(across)])  5.02 us
    ppermute x4, waiting for transfers between devices, exchange(): corners = [lax.ppermute(x, axes, p) for x, p in zip(near, pairs)]  4.8 us
    ppermute x2, waiting for transfers between devices, exchange(): lax.ppermute(pack, 'gx', [((g + 1) % across, g) for g in range(across)])  3.92 us
    ppermute x2, starting transfers between devices, exchange(): lax.ppermute(pack, 'gx', [(g, (g + 1) % across) for g in range(across)])  1.46 us
  transfers between devices with their start and end apart: 12, of which 5 were waited for; matrix products, arithmetic and copies ran while one was open for 0% of the time, Pallas kernels for 3%

profile of v2, /device:TPU:1, one launch (start us, length us, event | category | flops | bytes accessed | tf_op | source)
XLA Modules:
  0.0 71.1 jit_solution(17620756189227437644)
XLA Ops:
  0.6 3.3 %collective-permute-start.1 = (f32[792,128]{1,0:T(8,128)}, f32[792,128]{1,0:T(8,128)S(1)}, u32[]{:S(2)}, u32[]{:S(2)}) collective-permute-start(f32[792,128]{1,0:T(8,128)} %bitcast.10), channel_id=1, source_target_pairs={{0,32},{1,2},{2,1},{3,4},{4,3},{5,6},{6,5},{7,8},{8,7},{9,10},{10,... | collective-permute-start | bytes 1216520 | tf_op jit(solution)/shard_map/ppermute | solution.py:476
  4.0 0.9 %collective-permute-start = (f32[792,128]{1,0:T(8,128)}, f32[792,128]{1,0:T(8,128)S(1)}, u32[]{:S(2)}, u32[]{:S(2)}) collective-permute-start(f32[792,128]{1,0:T(8,128)} %bitcast.11), channel_id=1, source_target_pairs={{0,1},{1,0},{2,3},{3,2},{4,5},{5,4},{6,7},{7,6},{8,9},{9,8},{10,11... | collective-permute-start | bytes 1216520 | tf_op jit(solution)/shard_map/ppermute | solution.py:476
  4.8 1.4 %shard_map.59 = (f32[1064,128]{1,0:T(8,128)S(1)}, f32[288,128]{1,0:T(8,128)S(1)}, f32[288,128]{1,0:T(8,128)S(1)}, f32[80,128]{1,0:T(8,128)S(1)}, bf16[2,80,80]{2,1,0:T(8,128)(2,1)S(1)}) custom-call(f32[792,128]{1,0:T(8,128)} %bitcast.12, f32[264,128]{1,0:T(8,128)} %bitcast.13, f32[4,128]{1,0:T(4,128)} %relax.1, bf16[2,80,80]{2,1,0:T(8,128)(2,1)} %constant.70.clone.mats_in), custom_call_target="tpu_custom_call" | custom-call | tf_op jit(solution)/shard_map/pallas_call | solution.py:451
  6.2 1.2 %collective-permute-start.3 = (f32[80,128]{1,0:T(8,128)S(1)}, f32[80,128]{1,0:T(8,128)S(1)}, u32[]{:S(2)}, u32[]{:S(2)}) collective-permute-start(f32[80,128]{1,0:T(8,128)S(1)} %get-tuple-element.41.own_pack), channel_id=1, source_target_pairs={{32,0},{64,32},{96,64},{128,96},{160,128},{192,160},{224,192},{0,2... | collective-permute-start | bytes 122888 | tf_op jit(solution)/shard_map/ppermute | solution.py:478
  7.4 1.2 %collective-permute-start.2 = (f32[80,128]{1,0:T(8,128)S(1)}, f32[80,128]{1,0:T(8,128)S(1)}, u32[]{:S(2)}, u32[]{:S(2)}) collective-permute-start(f32[80,128]{1,0:T(8,128)S(1)} %get-tuple-element.41.own_pack), channel_id=1, source_target_pairs={{0,32},{32,64},{64,96},{96,128},{128,160},{160,192},{192,224},{224... | collective-permute-start | bytes 122888 | tf_op jit(solution)/shard_map/ppermute | solution.py:477
  8.6 1.9 %collective-permute-done.3 = f32[80,128]{1,0:T(8,128)S(1)} collective-permute-done((f32[80,128]{1,0:T(8,128)S(1)}, f32[80,128]{1,0:T(8,128)S(1)}, u32[]{:S(2)}, u32[]{:S(2)}) %collective-permute-start.3) | collective-permute-done | bytes 40992 | tf_op jit(solution)/shard_map/ppermute | solution.py:478
  10.6 0.0 collective-permute-done.2
  10.6 0.1 collective-permute-start.4
  10.7 3.6 %collective-permute-start.5 = (f32[288,128]{1,0:T(8,128)S(1)}, f32[288,128]{1,0:T(8,128)S(1)}, u32[]{:S(2)}, u32[]{:S(2)}) collective-permute-start(f32[288,128]{1,0:T(8,128)S(1)} %get-tuple-element.54), channel_id=1, source_target_pairs={{0,32},{1,2},{2,1},{3,4},{4,3},{5,6},{6,5},{7,8},{8,7},{9,10},{10,... | collective-permute-start | bytes 442376 | tf_op jit(solution)/shard_map/ppermute | solution.py:482
  14.4 2.5 %collective-permute-done.4.near_even = f32[288,128]{1,0:T(8,128)S(1)} collective-permute-done((f32[288,128]{1,0:T(8,128)S(1)}, f32[288,128]{1,0:T(8,128)S(1)}, u32[]{:S(2)}, u32[]{:S(2)}) %collective-permute-start.4) | collective-permute-done | bytes 147488 | tf_op jit(solution)/shard_map/ppermute | solution.py:482
  16.9 5.0 %shard_map.60 = (f32[792,128]{1,0:T(8,128)S(1)}, f32[80,128]{1,0:T(8,128)S(1)}, f32[4,792,128]{2,1,0:T(8,128)S(1)}, f32[2,12,40,128]{3,2,1,0:T(8,128)S(1)}, f32[2,2,40,128]{3,2,1,0:T(8,128)S(1)}) custom-call(f32[1064,128]{1,0:T(8,128)S(1)} %get-tuple-element.40.own, f32[80,128]{1,0:T(8,128)S(1)} %get-tuple-element.41.own_pack, ...), custom_call_target="tpu_custom_call" | custom-call | tf_op jit(solution)/shard_map/pallas_call | solution.py:451
  21.9 2.4 %collective-permute-start.7 = (f32[792,128]{1,0:T(8,128)S(1)}, f32[792,128]{1,0:T(8,128)S(1)}, u32[]{:S(2)}, u32[]{:S(2)}) collective-permute-start(f32[792,128]{1,0:T(8,128)S(1)} %get-tuple-element.45.main.own), channel_id=1, source_target_pairs={{0,32},{1,2},{2,1},{3,4},{4,3},{5,6},{6,5},{7,8},{8,7},{9,10},{10,... | collective-permute-start | bytes 1216520 | tf_op jit(solution)/shard_map/ppermute | solution.py:476
  24.4 1.6 %collective-permute-start.6 = (f32[792,128]{1,0:T(8,128)S(1)}, f32[792,128]{1,0:T(8,128)S(1)}, u32[]{:S(2)}, u32[]{:S(2)}) collective-permute-start(f32[792,128]{1,0:T(8,128)S(1)} %get-tuple-element.45.main.own), channel_id=1, source_target_pairs={{0,1},{1,0},{2,3},{3,2},{4,5},{5,4},{6,7},{7,6},{8,9},{9,8},{10,11... | collective-permute-start | bytes 1216520 | tf_op jit(solution)/shard_map/ppermute | solution.py:476
  25.9 3.8 %collective-permute-start.9 = (f32[80,128]{1,0:T(8,128)S(1)}, f32[80,128]{1,0:T(8,128)S(1)}, u32[]{:S(2)}, u32[]{:S(2)}) collective-permute-start(f32[80,128]{1,0:T(8,128)S(1)} %get-tuple-element.46.own_pack), channel_id=1, source_target_pairs={{32,0},{64,32},{96,64},{128,96},{160,128},{192,160},{224,192},{0,2... | collective-permute-start | bytes 122888 | tf_op jit(solution)/shard_map/ppermute | solution.py:478
  29.7 0.2 collective-permute-start.8
  29.9 2.0 %collective-permute-done.9 = f32[80,128]{1,0:T(8,128)S(1)} collective-permute-done((f32[80,128]{1,0:T(8,128)S(1)}, f32[80,128]{1,0:T(8,128)S(1)}, u32[]{:S(2)}, u32[]{:S(2)}) %collective-permute-start.9) | collective-permute-done | bytes 40992 | tf_op jit(solution)/shard_map/ppermute | solution.py:478
  31.9 2.6 %collective-permute-start.11 = (f32[80,128]{1,0:T(8,128)S(1)}, f32[80,128]{1,0:T(8,128)S(1)}, u32[]{:S(2)}, u32[]{:S(2)}) collective-permute-start(f32[80,128]{1,0:T(8,128)S(1)} %fusion.here), channel_id=1, source_target_pairs={{0,32},{1,2},{2,1},{3,4},{4,3},{5,6},{6,5},{7,8},{8,7},{9,10},{10,... | collective-permute-start | bytes 122888 | tf_op jit(solution)/shard_map/ppermute | solution.py:482
  34.5 0.1 collective-permute-start.10
  34.6 0.4 shard_map.61.early
  35.1 0.3 collective-permute-done.11.corner_odd
  35.4 2.0 %collective-permute-done.10.corner_even = f32[80,128]{1,0:T(8,128)S(1)} collective-permute-done((f32[80,128]{1,0:T(8,128)S(1)}, f32[80,128]{1,0:T(8,128)S(1)}, u32[]{:S(2)}, u32[]{:S(2)}) %collective-permute-start.10) | collective-permute-done | bytes 40992 | tf_op jit(solution)/shard_map/ppermute | solution.py:482
  37.4 5.9 %shard_map.62 = (f32[4,792,128]{2,1,0:T(8,128)S(1)}, f32[256,128]{1,0:T(8,128)S(1)}) custom-call(f32[792,128]{1,0:T(8,128)S(1)} %get-tuple-element.45.main.own, f32[80,128]{1,0:T(8,128)S(1)} %get-tuple-element.46.own_pack, f32[792,128]{1,0:T(8,128)S(1)} %collective-permute-done.6.even, f32[792,128]{1,0:T(8,128)S(1)} %collective-permute-done.7.odd, ...), custom_call_target="tpu_custom_call" | custom-call | tf_op jit(solution)/shard_map/pallas_call | solution.py:451
  43.3 26.1 %all_to_all.5 = f32[256,1,128]{2,1,0:T(1,128)S(1)} all-to-all(f32[256,1,128]{2,1,0:T(1,128)S(1)} %bitcast.9), channel_id=1, replica_groups=mesh['gx'=8,'gy'=32] {'gx','gy'}, dimensions={0} | all-to-all | bytes 262144 | tf_op jit(solution)/shard_map/all_to_all | solution.py:519
  69.4 1.6 %shard_map.63 = (f32[792,128]{1,0:T(8,128)}, f32[792,128]{1,0:T(8,128)}) custom-call(f32[256,128]{1,0:T(8,128)S(1)} %bitcast.8, f32[4,792,128]{2,1,0:T(8,128)S(1)} %get-tuple-element.49.older, f32[792,128]{1,0:T(8,128)S(1)} %get-tuple-element.45.main.own, f32[4,792,128]{2,1,0:T(8,128)S(1)} %get-tuple-element.51.newer), custom_call_target="tpu_custom_call" | custom-call | tf_op jit(solution)/shard_map/pallas_call | solution.py:451
  (11 shorter events, 0.0 us)
Async XLA Ops:
  0.6 16.2 %collective-permute-start.1 = (f32[792,128]{1,0:T(8,128)}, f32[792,128]{1,0:T(8,128)S(1)}, u32[]{:S(2)}, u32[]{:S(2)}) collective-permute-start(f32[792,128]{1,0:T(8,128)} %bitcast.10), channel_id=1, source_target_pairs={{0,32},{1,2},{2,1},{3,4},{4,3},{5,6},{6,5},{7,8},{8,7},{9,10},{10,... | collective-permute-start | bytes 1216520 | tf_op jit(solution)/shard_map/ppermute | solution.py:476
  4.0 12.9 %collective-permute-start = (f32[792,128]{1,0:T(8,128)}, f32[792,128]{1,0:T(8,128)S(1)}, u32[]{:S(2)}, u32[]{:S(2)}) collective-permute-start(f32[792,128]{1,0:T(8,128)} %bitcast.11), channel_id=1, source_target_pairs={{0,1},{1,0},{2,3},{3,2},{4,5},{5,4},{6,7},{7,6},{8,9},{9,8},{10,11... | collective-permute-start | bytes 1216520 | tf_op jit(solution)/shard_map/ppermute | solution.py:476
  6.2 4.4 %collective-permute-start.3 = (f32[80,128]{1,0:T(8,128)S(1)}, f32[80,128]{1,0:T(8,128)S(1)}, u32[]{:S(2)}, u32[]{:S(2)}) collective-permute-start(f32[80,128]{1,0:T(8,128)S(1)} %get-tuple-element.41.own_pack), channel_id=1, source_target_pairs={{32,0},{64,32},{96,64},{128,96},{160,128},{192,160},{224,192},{0,2... | collective-permute-start | bytes 122888 | tf_op jit(solution)/shard_map/ppermute | solution.py:478
  7.4 3.2 %collective-permute-start.2 = (f32[80,128]{1,0:T(8,128)S(1)}, f32[80,128]{1,0:T(8,128)S(1)}, u32[]{:S(2)}, u32[]{:S(2)}) collective-permute-start(f32[80,128]{1,0:T(8,128)S(1)} %get-tuple-element.41.own_pack), channel_id=1, source_target_pairs={{0,32},{32,64},{64,96},{96,128},{128,160},{160,192},{192,224},{224... | collective-permute-start | bytes 122888 | tf_op jit(solution)/shard_map/ppermute | solution.py:477
  10.6 6.2 %collective-permute-start.4 = (f32[288,128]{1,0:T(8,128)S(1)}, f32[288,128]{1,0:T(8,128)S(1)}, u32[]{:S(2)}, u32[]{:S(2)}) collective-permute-start(f32[288,128]{1,0:T(8,128)S(1)} %constant_dynamic-update-slice_fusion.1), channel_id=1, source_target_pairs={{0,1},{1,0},{2,3},{3,2},{4,5},{5,4},{6,7},{7,6},{8,9},{9,8},{10,11... | collective-permute-start | bytes 442376 | tf_op jit(solution)/shard_map/ppermute | solution.py:482
  10.7 6.1 %collective-permute-start.5 = (f32[288,128]{1,0:T(8,128)S(1)}, f32[288,128]{1,0:T(8,128)S(1)}, u32[]{:S(2)}, u32[]{:S(2)}) collective-permute-start(f32[288,128]{1,0:T(8,128)S(1)} %get-tuple-element.54), channel_id=1, source_target_pairs={{0,32},{1,2},{2,1},{3,4},{4,3},{5,6},{6,5},{7,8},{8,7},{9,10},{10,... | collective-permute-start | bytes 442376 | tf_op jit(solution)/shard_map/ppermute | solution.py:482
  21.9 15.4 %collective-permute-start.7 = (f32[792,128]{1,0:T(8,128)S(1)}, f32[792,128]{1,0:T(8,128)S(1)}, u32[]{:S(2)}, u32[]{:S(2)}) collective-permute-start(f32[792,128]{1,0:T(8,128)S(1)} %get-tuple-element.45.main.own), channel_id=1, source_target_pairs={{0,32},{1,2},{2,1},{3,4},{4,3},{5,6},{6,5},{7,8},{8,7},{9,10},{10,... | collective-permute-start | bytes 1216520 | tf_op jit(solution)/shard_map/ppermute | solution.py:476
  24.4 13.0 %collective-permute-start.6 = (f32[792,128]{1,0:T(8,128)S(1)}, f32[792,128]{1,0:T(8,128)S(1)}, u32[]{:S(2)}, u32[]{:S(2)}) collective-permute-start(f32[792,128]{1,0:T(8,128)S(1)} %get-tuple-element.45.main.own), channel_id=1, source_target_pairs={{0,1},{1,0},{2,3},{3,2},{4,5},{5,4},{6,7},{7,6},{8,9},{9,8},{10,11... | collective-permute-start | bytes 1216520 | tf_op jit(solution)/shard_map/ppermute | solution.py:476
  25.9 6.0 %collective-permute-start.9 = (f32[80,128]{1,0:T(8,128)S(1)}, f32[80,128]{1,0:T(8,128)S(1)}, u32[]{:S(2)}, u32[]{:S(2)}) collective-permute-start(f32[80,128]{1,0:T(8,128)S(1)} %get-tuple-element.46.own_pack), channel_id=1, source_target_pairs={{32,0},{64,32},{96,64},{128,96},{160,128},{192,160},{224,192},{0,2... | collective-permute-start | bytes 122888 | tf_op jit(solution)/shard_map/ppermute | solution.py:478
  29.7 2.2 %collective-permute-start.8 = (f32[80,128]{1,0:T(8,128)S(1)}, f32[80,128]{1,0:T(8,128)S(1)}, u32[]{:S(2)}, u32[]{:S(2)}) collective-permute-start(f32[80,128]{1,0:T(8,128)S(1)} %get-tuple-element.46.own_pack), channel_id=1, source_target_pairs={{0,32},{32,64},{64,96},{96,128},{128,160},{160,192},{192,224},{224... | collective-permute-start | bytes 122888 | tf_op jit(solution)/shard_map/ppermute | solution.py:477
  31.9 3.4 %collective-permute-start.11 = (f32[80,128]{1,0:T(8,128)S(1)}, f32[80,128]{1,0:T(8,128)S(1)}, u32[]{:S(2)}, u32[]{:S(2)}) collective-permute-start(f32[80,128]{1,0:T(8,128)S(1)} %fusion.here), channel_id=1, source_target_pairs={{0,32},{1,2},{2,1},{3,4},{4,3},{5,6},{6,5},{7,8},{8,7},{9,10},{10,... | collective-permute-start | bytes 122888 | tf_op jit(solution)/shard_map/ppermute | solution.py:482
  34.5 2.9 %collective-permute-start.10 = (f32[80,128]{1,0:T(8,128)S(1)}, f32[80,128]{1,0:T(8,128)S(1)}, u32[]{:S(2)}, u32[]{:S(2)}) collective-permute-start(f32[80,128]{1,0:T(8,128)S(1)} %fusion.here), channel_id=1, source_target_pairs={{0,1},{1,0},{2,3},{3,2},{4,5},{5,4},{6,7},{7,6},{8,9},{9,8},{10,11... | collective-permute-start | bytes 122888 | tf_op jit(solution)/shard_map/ppermute | solution.py:482

commit v3 on v2

--- a/solution.py
+++ b/solution.py
@@ -474,10 +474,10 @@
     pairs = trades(across, lax.axis_size("gy"))
     axes = ("gx", "gy")
     rows = [lax.ppermute(rows, axes, p) for p in pairs]
-    left = lax.ppermute(pack, "gx", [(g, (g + 1) % across) for g in range(across)])
-    right = lax.ppermute(pack, "gx", [((g + 1) % across, g) for g in range(across)])
+    ones = lax.ppermute(pack, "gx", [(g, g ^ 1) for g in range(across)])
+    others = lax.ppermute(pack, "gx", [(g, (g + (1 if g % 2 else -1)) % across) for g in range(across)])
     slot = lax.broadcasted_iota(jnp.int32, pack.shape, 1) % 8
-    here = jnp.where(slot < 4, left, right)
+    here = jnp.where((slot < 4) == (lax.axis_index("gx") % 2 == 1), ones, others)
     near = [x.at[:SIDE].set(here) for x in behind] or [here, here]
     corners = [lax.ppermute(x, axes, p) for x, p in zip(near, pairs)]
     return *rows, here, *corners

time: 71.3 us -> 71 us (level)
  starting transfers between devices: 21.1 us -> 18.4 us
  waiting for transfers between devices: 8.74 us -> 10.9 us
    ppermute x4, waiting for transfers between devices: 4.8 us -> 7.69 us  [exchange(): corners = [lax.ppermute(x, axes, p) for x, p in zip(near, pairs)]]
    ppermute x4, starting transfers between devices: 6.44 us -> 4.36 us  [exchange(): corners = [lax.ppermute(x, axes, p) for x, p in zip(near, pairs)]]
  transfers between devices with their start and end apart: 12 -> 12, of which waited for: 5 -> 4; matrix products, arithmetic and copies ran while one was open for 0% -> 0% of each run, Pallas kernels for 3% -> 3%
where the time goes in v3:
time: 71 us; the launch traced here: 70.8 us
  blocking collectives  26.4 us (37%)
  starting transfers between devices  18.4 us (26%)
  Pallas kernels  14.2 us (20%)
  waiting for transfers between devices  10.9 us (15%)
  between operations  0.86 us (1%)
    all_to_all x1, blocking collectives, shards(): lax.all_to_all(gram.reshape(PEERS, 1, 128), ('gx', 'gy'), 0, 0, tiled=True)  26.4 us
    pallas_call x5, Pallas kernels, call(): pl.pallas_call(kernel, out_shape=[make(shape, kind) for shape, kind in zi...  14.2 us
    ppermute x4, waiting for transfers between devices, exchange(): corners = [lax.ppermute(x, axes, p) for x, p in zip(near, pairs)]  7.69 us
    ppermute x4, starting transfers between devices, exchange(): rows = [lax.ppermute(rows, axes, p) for p in pairs]  7.52 us
    ppermute x2, starting transfers between devices, exchange(): lax.ppermute(pack, 'gx', [(g, (g + (1 if g % 2 else -1)) % across) for g...  5.8 us
    ppermute x4, starting transfers between devices, exchange(): corners = [lax.ppermute(x, axes, p) for x, p in zip(near, pairs)]  4.36 us
    ppermute x2, waiting for transfers between devices, exchange(): lax.ppermute(pack, 'gx', [(g, (g + (1 if g % 2 else -1)) % across) for g...  3.24 us
  transfers between devices with their start and end apart: 12, of which 4 were waited for; matrix products, arithmetic and copies ran while one was open for 0% of the time, Pallas kernels for 3%

profile of v3, /device:TPU:1, one launch (start us, length us, event | category | flops | bytes accessed | tf_op | source)
XLA Modules:
  0.0 70.8 jit_solution(2655627565711948473)
XLA Ops:
  0.6 3.3 %collective-permute-start.1 = (f32[792,128]{1,0:T(8,128)}, f32[792,128]{1,0:T(8,128)S(1)}, u32[]{:S(2)}, u32[]{:S(2)}) collective-permute-start(f32[792,128]{1,0:T(8,128)} %bitcast.10), channel_id=1, source_target_pairs={{0,32},{1,2},{2,1},{3,4},{4,3},{5,6},{6,5},{7,8},{8,7},{9,10},{10,... | collective-permute-start | bytes 1216520 | tf_op jit(solution)/shard_map/ppermute | solution.py:476
  4.0 0.9 %collective-permute-start = (f32[792,128]{1,0:T(8,128)}, f32[792,128]{1,0:T(8,128)S(1)}, u32[]{:S(2)}, u32[]{:S(2)}) collective-permute-start(f32[792,128]{1,0:T(8,128)} %bitcast.11), channel_id=1, source_target_pairs={{0,1},{1,0},{2,3},{3,2},{4,5},{5,4},{6,7},{7,6},{8,9},{9,8},{10,11... | collective-permute-start | bytes 1216520 | tf_op jit(solution)/shard_map/ppermute | solution.py:476
  4.8 1.4 %shard_map.59 = (f32[1064,128]{1,0:T(8,128)S(1)}, f32[288,128]{1,0:T(8,128)S(1)}, f32[288,128]{1,0:T(8,128)S(1)}, f32[80,128]{1,0:T(8,128)S(1)}, bf16[2,80,80]{2,1,0:T(8,128)(2,1)S(1)}) custom-call(f32[792,128]{1,0:T(8,128)} %bitcast.12, f32[264,128]{1,0:T(8,128)} %bitcast.13, f32[4,128]{1,0:T(4,128)} %relax.1, bf16[2,80,80]{2,1,0:T(8,128)(2,1)} %constant.91.clone.mats_in), custom_call_target="tpu_custom_call" | custom-call | tf_op jit(solution)/shard_map/pallas_call | solution.py:451
  6.2 2.5 %collective-permute-start.3 = (f32[80,128]{1,0:T(8,128)S(1)}, f32[80,128]{1,0:T(8,128)S(1)}, u32[]{:S(2)}, u32[]{:S(2)}) collective-permute-start(f32[80,128]{1,0:T(8,128)S(1)} %get-tuple-element.41.own_pack), channel_id=1, source_target_pairs={{0,224},{32,64},{64,32},{96,128},{128,96},{160,192},{192,160},{224... | collective-permute-start | bytes 122888 | tf_op jit(solution)/shard_map/ppermute | solution.py:478
  8.7 0.7 %collective-permute-start.2 = (f32[80,128]{1,0:T(8,128)S(1)}, f32[80,128]{1,0:T(8,128)S(1)}, u32[]{:S(2)}, u32[]{:S(2)}) collective-permute-start(f32[80,128]{1,0:T(8,128)S(1)} %get-tuple-element.41.own_pack), channel_id=1, source_target_pairs={{0,32},{32,0},{64,96},{96,64},{128,160},{160,128},{192,224},{224,1... | collective-permute-start | bytes 122888 | tf_op jit(solution)/shard_map/ppermute | solution.py:477
  9.4 1.3 %collective-permute-done.3 = f32[80,128]{1,0:T(8,128)S(1)} collective-permute-done((f32[80,128]{1,0:T(8,128)S(1)}, f32[80,128]{1,0:T(8,128)S(1)}, u32[]{:S(2)}, u32[]{:S(2)}) %collective-permute-start.3) | collective-permute-done | bytes 40992 | tf_op jit(solution)/shard_map/ppermute | solution.py:478
  10.7 0.1 collective-permute-start.4
  10.8 1.6 %collective-permute-start.5 = (f32[288,128]{1,0:T(8,128)S(1)}, f32[288,128]{1,0:T(8,128)S(1)}, u32[]{:S(2)}, u32[]{:S(2)}) collective-permute-start(f32[288,128]{1,0:T(8,128)S(1)} %get-tuple-element.54), channel_id=1, source_target_pairs={{0,32},{1,2},{2,1},{3,4},{4,3},{5,6},{6,5},{7,8},{8,7},{9,10},{10,... | collective-permute-start | bytes 442376 | tf_op jit(solution)/shard_map/ppermute | solution.py:482
  12.4 5.9 %collective-permute-done.4.near_even = f32[288,128]{1,0:T(8,128)S(1)} collective-permute-done((f32[288,128]{1,0:T(8,128)S(1)}, f32[288,128]{1,0:T(8,128)S(1)}, u32[]{:S(2)}, u32[]{:S(2)}) %collective-permute-start.4) | collective-permute-done | bytes 147488 | tf_op jit(solution)/shard_map/ppermute | solution.py:482
  18.3 0.0 collective-permute-done.1.odd
  18.3 0.0 collective-permute-done.even
  18.3 5.0 %shard_map.60 = (f32[792,128]{1,0:T(8,128)S(1)}, f32[80,128]{1,0:T(8,128)S(1)}, f32[4,792,128]{2,1,0:T(8,128)S(1)}, f32[2,12,40,128]{3,2,1,0:T(8,128)S(1)}, f32[2,2,40,128]{3,2,1,0:T(8,128)S(1)}) custom-call(f32[1064,128]{1,0:T(8,128)S(1)} %get-tuple-element.40.own, f32[80,128]{1,0:T(8,128)S(1)} %get-tuple-element.41.own_pack, ...), custom_call_target="tpu_custom_call" | custom-call | tf_op jit(solution)/shard_map/pallas_call | solution.py:451
  23.3 1.0 %collective-permute-start.7 = (f32[792,128]{1,0:T(8,128)S(1)}, f32[792,128]{1,0:T(8,128)S(1)}, u32[]{:S(2)}, u32[]{:S(2)}) collective-permute-start(f32[792,128]{1,0:T(8,128)S(1)} %get-tuple-element.45.main.own), channel_id=1, source_target_pairs={{0,32},{1,2},{2,1},{3,4},{4,3},{5,6},{6,5},{7,8},{8,7},{9,10},{10,... | collective-permute-start | bytes 1216520 | tf_op jit(solution)/shard_map/ppermute | solution.py:476
  24.3 2.4 %collective-permute-start.6 = (f32[792,128]{1,0:T(8,128)S(1)}, f32[792,128]{1,0:T(8,128)S(1)}, u32[]{:S(2)}, u32[]{:S(2)}) collective-permute-start(f32[792,128]{1,0:T(8,128)S(1)} %get-tuple-element.45.main.own), channel_id=1, source_target_pairs={{0,1},{1,0},{2,3},{3,2},{4,5},{5,4},{6,7},{7,6},{8,9},{9,8},{10,11... | collective-permute-start | bytes 1216520 | tf_op jit(solution)/shard_map/ppermute | solution.py:476
  26.6 3.3 %collective-permute-start.9 = (f32[80,128]{1,0:T(8,128)S(1)}, f32[80,128]{1,0:T(8,128)S(1)}, u32[]{:S(2)}, u32[]{:S(2)}) collective-permute-start(f32[80,128]{1,0:T(8,128)S(1)} %get-tuple-element.46.own_pack), channel_id=1, source_target_pairs={{0,224},{32,64},{64,32},{96,128},{128,96},{160,192},{192,160},{224... | collective-permute-start | bytes 122888 | tf_op jit(solution)/shard_map/ppermute | solution.py:478
  29.9 2.0 %collective-permute-done.9 = f32[80,128]{1,0:T(8,128)S(1)} collective-permute-done((f32[80,128]{1,0:T(8,128)S(1)}, f32[80,128]{1,0:T(8,128)S(1)}, u32[]{:S(2)}, u32[]{:S(2)}) %collective-permute-start.9) | collective-permute-done | bytes 40992 | tf_op jit(solution)/shard_map/ppermute | solution.py:478
  31.9 0.0 collective-permute-done.8
  31.9 1.6 %collective-permute-start.11 = (f32[80,128]{1,0:T(8,128)S(1)}, f32[80,128]{1,0:T(8,128)S(1)}, u32[]{:S(2)}, u32[]{:S(2)}) collective-permute-start(f32[80,128]{1,0:T(8,128)S(1)} %fusion.1.here), channel_id=1, source_target_pairs={{0,32},{1,2},{2,1},{3,4},{4,3},{5,6},{6,5},{7,8},{8,7},{9,10},{10,... | collective-permute-start | bytes 122888 | tf_op jit(solution)/shard_map/ppermute | solution.py:482
  33.5 1.1 %collective-permute-start.10 = (f32[80,128]{1,0:T(8,128)S(1)}, f32[80,128]{1,0:T(8,128)S(1)}, u32[]{:S(2)}, u32[]{:S(2)}) collective-permute-start(f32[80,128]{1,0:T(8,128)S(1)} %fusion.1.here), channel_id=1, source_target_pairs={{0,1},{1,0},{2,3},{3,2},{4,5},{5,4},{6,7},{7,6},{8,9},{9,8},{10,11... | collective-permute-start | bytes 122888 | tf_op jit(solution)/shard_map/ppermute | solution.py:482
  34.6 0.4 shard_map.61.early
  35.1 1.8 %collective-permute-done.10.corner_even = f32[80,128]{1,0:T(8,128)S(1)} collective-permute-done((f32[80,128]{1,0:T(8,128)S(1)}, f32[80,128]{1,0:T(8,128)S(1)}, u32[]{:S(2)}, u32[]{:S(2)}) %collective-permute-start.10) | collective-permute-done | bytes 40992 | tf_op jit(solution)/shard_map/ppermute | solution.py:482
  36.9 5.8 %shard_map.62 = (f32[4,792,128]{2,1,0:T(8,128)S(1)}, f32[256,128]{1,0:T(8,128)S(1)}) custom-call(f32[792,128]{1,0:T(8,128)S(1)} %get-tuple-element.45.main.own, f32[80,128]{1,0:T(8,128)S(1)} %get-tuple-element.46.own_pack, f32[792,128]{1,0:T(8,128)S(1)} %collective-permute-done.6.even, f32[792,128]{1,0:T(8,128)S(1)} %collective-permute-done.7.odd, ...), custom_call_target="tpu_custom_call" | custom-call | tf_op jit(solution)/shard_map/pallas_call | solution.py:451
  42.7 26.4 %all_to_all.5 = f32[256,1,128]{2,1,0:T(1,128)S(1)} all-to-all(f32[256,1,128]{2,1,0:T(1,128)S(1)} %bitcast.9), channel_id=1, replica_groups=mesh['gx'=8,'gy'=32] {'gx','gy'}, dimensions={0} | all-to-all | bytes 262144 | tf_op jit(solution)/shard_map/all_to_all | solution.py:519
  69.1 1.6 %shard_map.63 = (f32[792,128]{1,0:T(8,128)}, f32[792,128]{1,0:T(8,128)}) custom-call(f32[256,128]{1,0:T(8,128)S(1)} %bitcast.8, f32[4,792,128]{2,1,0:T(8,128)S(1)} %get-tuple-element.49.older, f32[792,128]{1,0:T(8,128)S(1)} %get-tuple-element.45.main.own, f32[4,792,128]{2,1,0:T(8,128)S(1)} %get-tuple-element.51.newer), custom_call_target="tpu_custom_call" | custom-call | tf_op jit(solution)/shard_map/pallas_call | solution.py:451
  (11 shorter events, 0.1 us)
Async XLA Ops:
  0.6 17.6 %collective-permute-start.1 = (f32[792,128]{1,0:T(8,128)}, f32[792,128]{1,0:T(8,128)S(1)}, u32[]{:S(2)}, u32[]{:S(2)}) collective-permute-start(f32[792,128]{1,0:T(8,128)} %bitcast.10), channel_id=1, source_target_pairs={{0,32},{1,2},{2,1},{3,4},{4,3},{5,6},{6,5},{7,8},{8,7},{9,10},{10,... | collective-permute-start | bytes 1216520 | tf_op jit(solution)/shard_map/ppermute | solution.py:476
  4.0 14.3 %collective-permute-start = (f32[792,128]{1,0:T(8,128)}, f32[792,128]{1,0:T(8,128)S(1)}, u32[]{:S(2)}, u32[]{:S(2)}) collective-permute-start(f32[792,128]{1,0:T(8,128)} %bitcast.11), channel_id=1, source_target_pairs={{0,1},{1,0},{2,3},{3,2},{4,5},{5,4},{6,7},{7,6},{8,9},{9,8},{10,11... | collective-permute-start | bytes 1216520 | tf_op jit(solution)/shard_map/ppermute | solution.py:476
  6.2 4.5 %collective-permute-start.3 = (f32[80,128]{1,0:T(8,128)S(1)}, f32[80,128]{1,0:T(8,128)S(1)}, u32[]{:S(2)}, u32[]{:S(2)}) collective-permute-start(f32[80,128]{1,0:T(8,128)S(1)} %get-tuple-element.41.own_pack), channel_id=1, source_target_pairs={{0,224},{32,64},{64,32},{96,128},{128,96},{160,192},{192,160},{224... | collective-permute-start | bytes 122888 | tf_op jit(solution)/shard_map/ppermute | solution.py:478
  8.7 2.0 %collective-permute-start.2 = (f32[80,128]{1,0:T(8,128)S(1)}, f32[80,128]{1,0:T(8,128)S(1)}, u32[]{:S(2)}, u32[]{:S(2)}) collective-permute-start(f32[80,128]{1,0:T(8,128)S(1)} %get-tuple-element.41.own_pack), channel_id=1, source_target_pairs={{0,32},{32,0},{64,96},{96,64},{128,160},{160,128},{192,224},{224,1... | collective-permute-start | bytes 122888 | tf_op jit(solution)/shard_map/ppermute | solution.py:477
  10.7 7.6 %collective-permute-start.4 = (f32[288,128]{1,0:T(8,128)S(1)}, f32[288,128]{1,0:T(8,128)S(1)}, u32[]{:S(2)}, u32[]{:S(2)}) collective-permute-start(f32[288,128]{1,0:T(8,128)S(1)} %constant_dynamic-update-slice_fusion.1), channel_id=1, source_target_pairs={{0,1},{1,0},{2,3},{3,2},{4,5},{5,4},{6,7},{7,6},{8,9},{9,8},{10,11... | collective-permute-start | bytes 442376 | tf_op jit(solution)/shard_map/ppermute | solution.py:482
  10.8 7.5 %collective-permute-start.5 = (f32[288,128]{1,0:T(8,128)S(1)}, f32[288,128]{1,0:T(8,128)S(1)}, u32[]{:S(2)}, u32[]{:S(2)}) collective-permute-start(f32[288,128]{1,0:T(8,128)S(1)} %get-tuple-element.54), channel_id=1, source_target_pairs={{0,32},{1,2},{2,1},{3,4},{4,3},{5,6},{6,5},{7,8},{8,7},{9,10},{10,... | collective-permute-start | bytes 442376 | tf_op jit(solution)/shard_map/ppermute | solution.py:482
  23.3 13.6 %collective-permute-start.7 = (f32[792,128]{1,0:T(8,128)S(1)}, f32[792,128]{1,0:T(8,128)S(1)}, u32[]{:S(2)}, u32[]{:S(2)}) collective-permute-start(f32[792,128]{1,0:T(8,128)S(1)} %get-tuple-element.45.main.own), channel_id=1, source_target_pairs={{0,32},{1,2},{2,1},{3,4},{4,3},{5,6},{6,5},{7,8},{8,7},{9,10},{10,... | collective-permute-start | bytes 1216520 | tf_op jit(solution)/shard_map/ppermute | solution.py:476
  24.3 12.6 %collective-permute-start.6 = (f32[792,128]{1,0:T(8,128)S(1)}, f32[792,128]{1,0:T(8,128)S(1)}, u32[]{:S(2)}, u32[]{:S(2)}) collective-permute-start(f32[792,128]{1,0:T(8,128)S(1)} %get-tuple-element.45.main.own), channel_id=1, source_target_pairs={{0,1},{1,0},{2,3},{3,2},{4,5},{5,4},{6,7},{7,6},{8,9},{9,8},{10,11... | collective-permute-start | bytes 1216520 | tf_op jit(solution)/shard_map/ppermute | solution.py:476
  26.6 5.3 %collective-permute-start.9 = (f32[80,128]{1,0:T(8,128)S(1)}, f32[80,128]{1,0:T(8,128)S(1)}, u32[]{:S(2)}, u32[]{:S(2)}) collective-permute-start(f32[80,128]{1,0:T(8,128)S(1)} %get-tuple-element.46.own_pack), channel_id=1, source_target_pairs={{0,224},{32,64},{64,32},{96,128},{128,96},{160,192},{192,160},{224... | collective-permute-start | bytes 122888 | tf_op jit(solution)/shard_map/ppermute | solution.py:478
  29.9 2.0 %collective-permute-start.8 = (f32[80,128]{1,0:T(8,128)S(1)}, f32[80,128]{1,0:T(8,128)S(1)}, u32[]{:S(2)}, u32[]{:S(2)}) collective-permute-start(f32[80,128]{1,0:T(8,128)S(1)} %get-tuple-element.46.own_pack), channel_id=1, source_target_pairs={{0,32},{32,0},{64,96},{96,64},{128,160},{160,128},{192,224},{224,1... | collective-permute-start | bytes 122888 | tf_op jit(solution)/shard_map/ppermute | solution.py:477
  31.9 3.1 %collective-permute-start.11 = (f32[80,128]{1,0:T(8,128)S(1)}, f32[80,128]{1,0:T(8,128)S(1)}, u32[]{:S(2)}, u32[]{:S(2)}) collective-permute-start(f32[80,128]{1,0:T(8,128)S(1)} %fusion.1.here), channel_id=1, source_target_pairs={{0,32},{1,2},{2,1},{3,4},{4,3},{5,6},{6,5},{7,8},{8,7},{9,10},{10,... | collective-permute-start | bytes 122888 | tf_op jit(solution)/shard_map/ppermute | solution.py:482
  33.5 3.4 %collective-permute-start.10 = (f32[80,128]{1,0:T(8,128)S(1)}, f32[80,128]{1,0:T(8,128)S(1)}, u32[]{:S(2)}, u32[]{:S(2)}) collective-permute-start(f32[80,128]{1,0:T(8,128)S(1)} %fusion.1.here), channel_id=1, source_target_pairs={{0,1},{1,0},{2,3},{3,2},{4,5},{5,4},{6,7},{7,6},{8,9},{9,8},{10,11... | collective-permute-start | bytes 122888 | tf_op jit(solution)/shard_map/ppermute | solution.py:482

commit v4 on v3

--- a/solution.py
+++ b/solution.py
@@ -45,6 +45,10 @@
 
 def lanes(shape=(1, 128)):
     return lax.broadcasted_iota(jnp.int32, shape, len(shape) - 1)
+
+
+def turned(x, by):
+    return pltpu.roll(x, by % 128, 1) if by % 128 else x
 
 
 def window(x, place):
@@ -120,7 +124,7 @@
 def sides_of(dst, f, own, sides, g, j, ok):
     lane = lanes()
     north, here, south = (
-        pltpu.roll(ref[g][...], (base - 32 * j) % 128, 1) for base, ref in zip((0, 32, 64), sides)
+        turned(ref[g][...], base - 32 * j) for base, ref in zip((0, 32, 64), sides)
     )
     halo = jnp.where(lane < 32, north, jnp.where(lane < 64, here, south))
     slot = lane % 8
@@ -130,7 +134,7 @@
 
 def own_windows(slab, pack, f, scale=None):
     lane = lanes()
-    here = pltpu.roll(pack[pl.ds(f // 4 * TP, TP)], (8 * H - 32 * (f % 4)) % 128, 1)
+    here = turned(pack[pl.ds(f // 4 * TP, TP)], 8 * H - 32 * (f % 4))
     total = jnp.where((lane >= 8 * H) & (lane < 8 * (H + R)), here if scale is None else here * scale, 0.0)
     for e in range(1, E - 1):
         if not H <= e < H + R:

time: 71 us -> 71 us (level)
  no operation moved by 1% of the time
where the time goes in v4:
time: 71 us; the launch traced here: 70.8 us
  blocking collectives  26.4 us (37%)
  starting transfers between devices  18.4 us (26%)
  Pallas kernels  14.2 us (20%)
  waiting for transfers between devices  10.9 us (15%)
  between operations  0.86 us (1%)
    all_to_all x1, blocking collectives, shards(): lax.all_to_all(gram.reshape(PEERS, 1, 128), ('gx', 'gy'), 0, 0, tiled=True)  26.4 us
    pallas_call x5, Pallas kernels, call(): pl.pallas_call(kernel, out_shape=[make(shape, kind) for shape, kind in zi...  14.2 us
    ppermute x4, waiting for transfers between devices, exchange(): corners = [lax.ppermute(x, axes, p) for x, p in zip(near, pairs)]  7.69 us
    ppermute x4, starting transfers between devices, exchange(): rows = [lax.ppermute(rows, axes, p) for p in pairs]  7.52 us
    ppermute x2, starting transfers between devices, exchange(): lax.ppermute(pack, 'gx', [(g, (g + (1 if g % 2 else -1)) % across) for g...  5.8 us
    ppermute x4, starting transfers between devices, exchange(): corners = [lax.ppermute(x, axes, p) for x, p in zip(near, pairs)]  4.36 us
    ppermute x2, waiting for transfers between devices, exchange(): lax.ppermute(pack, 'gx', [(g, (g + (1 if g % 2 else -1)) % across) for g...  3.24 us
  transfers between devices with their start and end apart: 12, of which 4 were waited for; matrix products, arithmetic and copies ran while one was open for 0% of the time, Pallas kernels for 3%

profile of v4, /device:TPU:1, one launch (start us, length us, event | category | flops | bytes accessed | tf_op | source)
XLA Modules:
  0.0 70.8 jit_solution(2655627565711948473)
XLA Ops:
  0.6 3.3 %collective-permute-start.1 = (f32[792,128]{1,0:T(8,128)}, f32[792,128]{1,0:T(8,128)S(1)}, u32[]{:S(2)}, u32[]{:S(2)}) collective-permute-start(f32[792,128]{1,0:T(8,128)} %bitcast.10), channel_id=1, source_target_pairs={{0,32},{1,2},{2,1},{3,4},{4,3},{5,6},{6,5},{7,8},{8,7},{9,10},{10,... | collective-permute-start | bytes 1216520 | tf_op jit(solution)/shard_map/ppermute | solution.py:480
  4.0 0.9 %collective-permute-start = (f32[792,128]{1,0:T(8,128)}, f32[792,128]{1,0:T(8,128)S(1)}, u32[]{:S(2)}, u32[]{:S(2)}) collective-permute-start(f32[792,128]{1,0:T(8,128)} %bitcast.11), channel_id=1, source_target_pairs={{0,1},{1,0},{2,3},{3,2},{4,5},{5,4},{6,7},{7,6},{8,9},{9,8},{10,11... | collective-permute-start | bytes 1216520 | tf_op jit(solution)/shard_map/ppermute | solution.py:480
  4.8 1.4 %shard_map.59 = (f32[1064,128]{1,0:T(8,128)S(1)}, f32[288,128]{1,0:T(8,128)S(1)}, f32[288,128]{1,0:T(8,128)S(1)}, f32[80,128]{1,0:T(8,128)S(1)}, bf16[2,80,80]{2,1,0:T(8,128)(2,1)S(1)}) custom-call(f32[792,128]{1,0:T(8,128)} %bitcast.12, f32[264,128]{1,0:T(8,128)} %bitcast.13, f32[4,128]{1,0:T(4,128)} %relax.1, bf16[2,80,80]{2,1,0:T(8,128)(2,1)} %constant.91.clone.mats_in), custom_call_target="tpu_custom_call" | custom-call | tf_op jit(solution)/shard_map/pallas_call | solution.py:455
  6.2 2.5 %collective-permute-start.3 = (f32[80,128]{1,0:T(8,128)S(1)}, f32[80,128]{1,0:T(8,128)S(1)}, u32[]{:S(2)}, u32[]{:S(2)}) collective-permute-start(f32[80,128]{1,0:T(8,128)S(1)} %get-tuple-element.41.own_pack), channel_id=1, source_target_pairs={{0,224},{32,64},{64,32},{96,128},{128,96},{160,192},{192,160},{224... | collective-permute-start | bytes 122888 | tf_op jit(solution)/shard_map/ppermute | solution.py:482
  8.7 0.7 %collective-permute-start.2 = (f32[80,128]{1,0:T(8,128)S(1)}, f32[80,128]{1,0:T(8,128)S(1)}, u32[]{:S(2)}, u32[]{:S(2)}) collective-permute-start(f32[80,128]{1,0:T(8,128)S(1)} %get-tuple-element.41.own_pack), channel_id=1, source_target_pairs={{0,32},{32,0},{64,96},{96,64},{128,160},{160,128},{192,224},{224,1... | collective-permute-start | bytes 122888 | tf_op jit(solution)/shard_map/ppermute | solution.py:481
  9.4 1.3 %collective-permute-done.3 = f32[80,128]{1,0:T(8,128)S(1)} collective-permute-done((f32[80,128]{1,0:T(8,128)S(1)}, f32[80,128]{1,0:T(8,128)S(1)}, u32[]{:S(2)}, u32[]{:S(2)}) %collective-permute-start.3) | collective-permute-done | bytes 40992 | tf_op jit(solution)/shard_map/ppermute | solution.py:482
  10.7 0.1 collective-permute-start.4
  10.8 1.6 %collective-permute-start.5 = (f32[288,128]{1,0:T(8,128)S(1)}, f32[288,128]{1,0:T(8,128)S(1)}, u32[]{:S(2)}, u32[]{:S(2)}) collective-permute-start(f32[288,128]{1,0:T(8,128)S(1)} %get-tuple-element.54), channel_id=1, source_target_pairs={{0,32},{1,2},{2,1},{3,4},{4,3},{5,6},{6,5},{7,8},{8,7},{9,10},{10,... | collective-permute-start | bytes 442376 | tf_op jit(solution)/shard_map/ppermute | solution.py:486
  12.4 5.9 %collective-permute-done.4.near_even = f32[288,128]{1,0:T(8,128)S(1)} collective-permute-done((f32[288,128]{1,0:T(8,128)S(1)}, f32[288,128]{1,0:T(8,128)S(1)}, u32[]{:S(2)}, u32[]{:S(2)}) %collective-permute-start.4) | collective-permute-done | bytes 147488 | tf_op jit(solution)/shard_map/ppermute | solution.py:486
  18.3 0.0 collective-permute-done.1.odd
  18.3 0.0 collective-permute-done.even
  18.3 5.0 %shard_map.60 = (f32[792,128]{1,0:T(8,128)S(1)}, f32[80,128]{1,0:T(8,128)S(1)}, f32[4,792,128]{2,1,0:T(8,128)S(1)}, f32[2,12,40,128]{3,2,1,0:T(8,128)S(1)}, f32[2,2,40,128]{3,2,1,0:T(8,128)S(1)}) custom-call(f32[1064,128]{1,0:T(8,128)S(1)} %get-tuple-element.40.own, f32[80,128]{1,0:T(8,128)S(1)} %get-tuple-element.41.own_pack, ...), custom_call_target="tpu_custom_call" | custom-call | tf_op jit(solution)/shard_map/pallas_call | solution.py:455
  23.3 1.0 %collective-permute-start.7 = (f32[792,128]{1,0:T(8,128)S(1)}, f32[792,128]{1,0:T(8,128)S(1)}, u32[]{:S(2)}, u32[]{:S(2)}) collective-permute-start(f32[792,128]{1,0:T(8,128)S(1)} %get-tuple-element.45.main.own), channel_id=1, source_target_pairs={{0,32},{1,2},{2,1},{3,4},{4,3},{5,6},{6,5},{7,8},{8,7},{9,10},{10,... | collective-permute-start | bytes 1216520 | tf_op jit(solution)/shard_map/ppermute | solution.py:480
  24.3 2.4 %collective-permute-start.6 = (f32[792,128]{1,0:T(8,128)S(1)}, f32[792,128]{1,0:T(8,128)S(1)}, u32[]{:S(2)}, u32[]{:S(2)}) collective-permute-start(f32[792,128]{1,0:T(8,128)S(1)} %get-tuple-element.45.main.own), channel_id=1, source_target_pairs={{0,1},{1,0},{2,3},{3,2},{4,5},{5,4},{6,7},{7,6},{8,9},{9,8},{10,11... | collective-permute-start | bytes 1216520 | tf_op jit(solution)/shard_map/ppermute | solution.py:480
  26.6 3.3 %collective-permute-start.9 = (f32[80,128]{1,0:T(8,128)S(1)}, f32[80,128]{1,0:T(8,128)S(1)}, u32[]{:S(2)}, u32[]{:S(2)}) collective-permute-start(f32[80,128]{1,0:T(8,128)S(1)} %get-tuple-element.46.own_pack), channel_id=1, source_target_pairs={{0,224},{32,64},{64,32},{96,128},{128,96},{160,192},{192,160},{224... | collective-permute-start | bytes 122888 | tf_op jit(solution)/shard_map/ppermute | solution.py:482
  29.9 2.0 %collective-permute-done.9 = f32[80,128]{1,0:T(8,128)S(1)} collective-permute-done((f32[80,128]{1,0:T(8,128)S(1)}, f32[80,128]{1,0:T(8,128)S(1)}, u32[]{:S(2)}, u32[]{:S(2)}) %collective-permute-start.9) | collective-permute-done | bytes 40992 | tf_op jit(solution)/shard_map/ppermute | solution.py:482
  31.9 0.0 collective-permute-done.8
  31.9 1.6 %collective-permute-start.11 = (f32[80,128]{1,0:T(8,128)S(1)}, f32[80,128]{1,0:T(8,128)S(1)}, u32[]{:S(2)}, u32[]{:S(2)}) collective-permute-start(f32[80,128]{1,0:T(8,128)S(1)} %fusion.1.here), channel_id=1, source_target_pairs={{0,32},{1,2},{2,1},{3,4},{4,3},{5,6},{6,5},{7,8},{8,7},{9,10},{10,... | collective-permute-start | bytes 122888 | tf_op jit(solution)/shard_map/ppermute | solution.py:486
  33.5 1.1 %collective-permute-start.10 = (f32[80,128]{1,0:T(8,128)S(1)}, f32[80,128]{1,0:T(8,128)S(1)}, u32[]{:S(2)}, u32[]{:S(2)}) collective-permute-start(f32[80,128]{1,0:T(8,128)S(1)} %fusion.1.here), channel_id=1, source_target_pairs={{0,1},{1,0},{2,3},{3,2},{4,5},{5,4},{6,7},{7,6},{8,9},{9,8},{10,11... | collective-permute-start | bytes 122888 | tf_op jit(solution)/shard_map/ppermute | solution.py:486
  34.6 0.4 shard_map.61.early
  35.1 1.8 %collective-permute-done.10.corner_even = f32[80,128]{1,0:T(8,128)S(1)} collective-permute-done((f32[80,128]{1,0:T(8,128)S(1)}, f32[80,128]{1,0:T(8,128)S(1)}, u32[]{:S(2)}, u32[]{:S(2)}) %collective-permute-start.10) | collective-permute-done | bytes 40992 | tf_op jit(solution)/shard_map/ppermute | solution.py:486
  36.9 5.8 %shard_map.62 = (f32[4,792,128]{2,1,0:T(8,128)S(1)}, f32[256,128]{1,0:T(8,128)S(1)}) custom-call(f32[792,128]{1,0:T(8,128)S(1)} %get-tuple-element.45.main.own, f32[80,128]{1,0:T(8,128)S(1)} %get-tuple-element.46.own_pack, f32[792,128]{1,0:T(8,128)S(1)} %collective-permute-done.6.even, f32[792,128]{1,0:T(8,128)S(1)} %collective-permute-done.7.odd, ...), custom_call_target="tpu_custom_call" | custom-call | tf_op jit(solution)/shard_map/pallas_call | solution.py:455
  42.7 26.4 %all_to_all.5 = f32[256,1,128]{2,1,0:T(1,128)S(1)} all-to-all(f32[256,1,128]{2,1,0:T(1,128)S(1)} %bitcast.9), channel_id=1, replica_groups=mesh['gx'=8,'gy'=32] {'gx','gy'}, dimensions={0} | all-to-all | bytes 262144 | tf_op jit(solution)/shard_map/all_to_all | solution.py:523
  69.1 1.6 %shard_map.63 = (f32[792,128]{1,0:T(8,128)}, f32[792,128]{1,0:T(8,128)}) custom-call(f32[256,128]{1,0:T(8,128)S(1)} %bitcast.8, f32[4,792,128]{2,1,0:T(8,128)S(1)} %get-tuple-element.49.older, f32[792,128]{1,0:T(8,128)S(1)} %get-tuple-element.45.main.own, f32[4,792,128]{2,1,0:T(8,128)S(1)} %get-tuple-element.51.newer), custom_call_target="tpu_custom_call" | custom-call | tf_op jit(solution)/shard_map/pallas_call | solution.py:455
  (11 shorter events, 0.1 us)
Async XLA Ops:
  0.6 17.6 %collective-permute-start.1 = (f32[792,128]{1,0:T(8,128)}, f32[792,128]{1,0:T(8,128)S(1)}, u32[]{:S(2)}, u32[]{:S(2)}) collective-permute-start(f32[792,128]{1,0:T(8,128)} %bitcast.10), channel_id=1, source_target_pairs={{0,32},{1,2},{2,1},{3,4},{4,3},{5,6},{6,5},{7,8},{8,7},{9,10},{10,... | collective-permute-start | bytes 1216520 | tf_op jit(solution)/shard_map/ppermute | solution.py:480
  4.0 14.3 %collective-permute-start = (f32[792,128]{1,0:T(8,128)}, f32[792,128]{1,0:T(8,128)S(1)}, u32[]{:S(2)}, u32[]{:S(2)}) collective-permute-start(f32[792,128]{1,0:T(8,128)} %bitcast.11), channel_id=1, source_target_pairs={{0,1},{1,0},{2,3},{3,2},{4,5},{5,4},{6,7},{7,6},{8,9},{9,8},{10,11... | collective-permute-start | bytes 1216520 | tf_op jit(solution)/shard_map/ppermute | solution.py:480
  6.2 4.5 %collective-permute-start.3 = (f32[80,128]{1,0:T(8,128)S(1)}, f32[80,128]{1,0:T(8,128)S(1)}, u32[]{:S(2)}, u32[]{:S(2)}) collective-permute-start(f32[80,128]{1,0:T(8,128)S(1)} %get-tuple-element.41.own_pack), channel_id=1, source_target_pairs={{0,224},{32,64},{64,32},{96,128},{128,96},{160,192},{192,160},{224... | collective-permute-start | bytes 122888 | tf_op jit(solution)/shard_map/ppermute | solution.py:482
  8.7 2.0 %collective-permute-start.2 = (f32[80,128]{1,0:T(8,128)S(1)}, f32[80,128]{1,0:T(8,128)S(1)}, u32[]{:S(2)}, u32[]{:S(2)}) collective-permute-start(f32[80,128]{1,0:T(8,128)S(1)} %get-tuple-element.41.own_pack), channel_id=1, source_target_pairs={{0,32},{32,0},{64,96},{96,64},{128,160},{160,128},{192,224},{224,1... | collective-permute-start | bytes 122888 | tf_op jit(solution)/shard_map/ppermute | solution.py:481
  10.7 7.6 %collective-permute-start.4 = (f32[288,128]{1,0:T(8,128)S(1)}, f32[288,128]{1,0:T(8,128)S(1)}, u32[]{:S(2)}, u32[]{:S(2)}) collective-permute-start(f32[288,128]{1,0:T(8,128)S(1)} %constant_dynamic-update-slice_fusion.1), channel_id=1, source_target_pairs={{0,1},{1,0},{2,3},{3,2},{4,5},{5,4},{6,7},{7,6},{8,9},{9,8},{10,11... | collective-permute-start | bytes 442376 | tf_op jit(solution)/shard_map/ppermute | solution.py:486
  10.8 7.5 %collective-permute-start.5 = (f32[288,128]{1,0:T(8,128)S(1)}, f32[288,128]{1,0:T(8,128)S(1)}, u32[]{:S(2)}, u32[]{:S(2)}) collective-permute-start(f32[288,128]{1,0:T(8,128)S(1)} %get-tuple-element.54), channel_id=1, source_target_pairs={{0,32},{1,2},{2,1},{3,4},{4,3},{5,6},{6,5},{7,8},{8,7},{9,10},{10,... | collective-permute-start | bytes 442376 | tf_op jit(solution)/shard_map/ppermute | solution.py:486
  23.3 13.6 %collective-permute-start.7 = (f32[792,128]{1,0:T(8,128)S(1)}, f32[792,128]{1,0:T(8,128)S(1)}, u32[]{:S(2)}, u32[]{:S(2)}) collective-permute-start(f32[792,128]{1,0:T(8,128)S(1)} %get-tuple-element.45.main.own), channel_id=1, source_target_pairs={{0,32},{1,2},{2,1},{3,4},{4,3},{5,6},{6,5},{7,8},{8,7},{9,10},{10,... | collective-permute-start | bytes 1216520 | tf_op jit(solution)/shard_map/ppermute | solution.py:480
  24.3 12.6 %collective-permute-start.6 = (f32[792,128]{1,0:T(8,128)S(1)}, f32[792,128]{1,0:T(8,128)S(1)}, u32[]{:S(2)}, u32[]{:S(2)}) collective-permute-start(f32[792,128]{1,0:T(8,128)S(1)} %get-tuple-element.45.main.own), channel_id=1, source_target_pairs={{0,1},{1,0},{2,3},{3,2},{4,5},{5,4},{6,7},{7,6},{8,9},{9,8},{10,11... | collective-permute-start | bytes 1216520 | tf_op jit(solution)/shard_map/ppermute | solution.py:480
  26.6 5.3 %collective-permute-start.9 = (f32[80,128]{1,0:T(8,128)S(1)}, f32[80,128]{1,0:T(8,128)S(1)}, u32[]{:S(2)}, u32[]{:S(2)}) collective-permute-start(f32[80,128]{1,0:T(8,128)S(1)} %get-tuple-element.46.own_pack), channel_id=1, source_target_pairs={{0,224},{32,64},{64,32},{96,128},{128,96},{160,192},{192,160},{224... | collective-permute-start | bytes 122888 | tf_op jit(solution)/shard_map/ppermute | solution.py:482
  29.9 2.0 %collective-permute-start.8 = (f32[80,128]{1,0:T(8,128)S(1)}, f32[80,128]{1,0:T(8,128)S(1)}, u32[]{:S(2)}, u32[]{:S(2)}) collective-permute-start(f32[80,128]{1,0:T(8,128)S(1)} %get-tuple-element.46.own_pack), channel_id=1, source_target_pairs={{0,32},{32,0},{64,96},{96,64},{128,160},{160,128},{192,224},{224,1... | collective-permute-start | bytes 122888 | tf_op jit(solution)/shard_map/ppermute | solution.py:481
  31.9 3.1 %collective-permute-start.11 = (f32[80,128]{1,0:T(8,128)S(1)}, f32[80,128]{1,0:T(8,128)S(1)}, u32[]{:S(2)}, u32[]{:S(2)}) collective-permute-start(f32[80,128]{1,0:T(8,128)S(1)} %fusion.1.here), channel_id=1, source_target_pairs={{0,32},{1,2},{2,1},{3,4},{4,3},{5,6},{6,5},{7,8},{8,7},{9,10},{10,... | collective-permute-start | bytes 122888 | tf_op jit(solution)/shard_map/ppermute | solution.py:486
  33.5 3.4 %collective-permute-start.10 = (f32[80,128]{1,0:T(8,128)S(1)}, f32[80,128]{1,0:T(8,128)S(1)}, u32[]{:S(2)}, u32[]{:S(2)}) collective-permute-start(f32[80,128]{1,0:T(8,128)S(1)} %fusion.1.here), channel_id=1, source_target_pairs={{0,1},{1,0},{2,3},{3,2},{4,5},{5,4},{6,7},{7,6},{8,9},{9,8},{10,11... | collective-permute-start | bytes 122888 | tf_op jit(solution)/shard_map/ppermute | solution.py:486
